TPU v7x, 512 devices: a whole 4x4x16 slice. The times are simulated.
512 devices in a mesh: samp: 16 (over z_hi, x), feat: 32 (over y, z_lo, core).
Axes of the slice: x: 4, y: 4, z: 16 (z_hi: 4, z_lo: 4; z = z_hi * 4 + z_lo), core: 2. Of those that a mesh axis runs over, the one named last changes fastest.
Arguments:
- design: bfloat16 [3072, 262144], P('samp', 'feat'), may hold values from -6 to 6
- weights: float32 [3072], P('samp'), may hold values from 0.01 to 0.25
- probes: bfloat16 [262144, 64], P('feat'), may hold values from -0.01171875 to 0.01171875
- barrier: float32 [262144], P(('feat', 'samp')), may hold values from 200 to 4000
Outputs:
- sketch: float32 [262144, 64], P(('feat', 'samp'))
All inputs are finite; a program needn't handle non-finite values.
Results may differ from a plain program's by a relative error of at most 0.00075.
Values may be sent and summed in bfloat16 or wider, within the bound.
No kernel may reach another device: no remote copies, remote signals or barrier semaphores. Data moves between devices by JAX's collectives and lax.ppermute only.
A program may use at most 64 MiB of HBM per device.

v0:
```python
import jax
import jax.numpy as jnp
from jax import lax
from jax.sharding import PartitionSpec as P


def per_device(design, weights, probes, barrier):
    partial_sums = jnp.dot(design, probes, preferred_element_type=jnp.float32)
    projected = lax.psum(partial_sums, "feat")
    scaled = (weights[:, None] * projected).astype(jnp.bfloat16)
    owned = probes.shape[0] // lax.axis_size("samp")
    summed = lax.psum_scatter(
        lax.dot_general(
            design, scaled, (((0,), (0,)), ((), ())), preferred_element_type=jnp.float32
        ),
        "samp",
        scatter_dimension=0,
        tiled=True,
    )
    own_probes = lax.dynamic_slice_in_dim(probes, lax.axis_index("samp") * owned, owned, 0)
    return summed + barrier[:, None] * own_probes.astype(jnp.float32)


def solution(mesh):
    placed = (P("samp", "feat"), P("samp"), P("feat", None), P(("feat", "samp")))
    return jax.shard_map(
        per_device, mesh=mesh, in_specs=placed, out_specs=P(("feat", "samp"), None), check_vma=False
    )
```

profile of v0, /device:TPU:1, one launch (start us, length us, event | category | flops | bytes accessed | tf_op | source)
XLA Modules:
  0.0 286.6 jit_solution(9488700240064446715)
XLA Ops:
  6.5 0.0 copy-start
  6.5 0.0 copy-start.2
  6.5 0.0 reduce-scatter.2.cloned.1.call-start
  6.5 1.9 copy-done
  8.4 2.2 fusion.1
  10.6 135.1 %psum.7 = f32[192,64]{1,0:T(8,128)S(1)} all-reduce(f32[192,64]{1,0:T(8,128)S(1)} %fusion.1), channel_id=1, replica_groups=mesh['samp'=16,'feat'=32] {'feat'}, use_global_device_ids=true, to_apply=%region_0.0 | all-reduce | flops 12288 | bytes 98304 | tf_op jit(solution)/shard_map/psum | solution.py:9
  145.7 0.0 copy-done.2
  145.7 0.0 copy-start.1
  145.7 2.2 convolution_bitcast_fusion
  147.8 0.0 reduce-scatter.2.cloned.1.call-update
  147.9 130.3 %reduce-scatter.2.cloned.1.call-done = f32[512,64]{0,1:T(8,128)} async-done(((f32[8192,64]{0,1:T(8,128)}), f32[512,64]{0,1:T(8,128)}) %reduce-scatter.2.cloned.1.call-update) | async-done | bytes 131088 | tf_op jit(solution)/shard_map/reduce_scatter | solution.py:12
  278.2 0.0 copy-done.1
  278.2 1.6 multiply_add_fusion
Async XLA Ops:
  6.5 1.9 copy-start
  6.5 139.1 %copy-start.2 = (f32[192]{0:T(256)S(1)}, f32[192]{0:T(256)}, u32[]{:S(2)}) copy-start(f32[192]{0:T(256)} %param.5) | copy-start | bytes 2308
  6.5 271.6 %reduce-scatter.2.cloned.1.call-start = ((), (), s32[]{:S(2)}) async-start(), calls=%async_computation.1 | async-start | bytes 2228224 | tf_op jit(solution)/shard_map/reduce_scatter | solution.py:12
  145.7 132.5 %copy-start.1 = (f32[512]{0:T(512)S(1)}, f32[512]{0:T(512)}, u32[]{:S(2)}) copy-start(f32[512]{0:T(512)} %param.7) | copy-start | bytes 6148
Sparse Core Ops, SparseCore 0:
  148.0 130.1 reduce-scatter.1
where the time goes:
time: 287 us
  blocking collectives  135 us (47%)
  waiting for transfers between devices  130 us (45%)
  between operations  13.4 us (5%)
  matrix products  4.35 us (2%)
    psum x1, blocking collectives, per_device(): projected = lax.psum(partial_sums, 'feat')  135 us
    reduce_scatter x1, waiting for transfers between devices, per_device(): lax.psum_scatter(lax.dot_general(design, scaled, (((0,), (0,)), ((), ()))...  130 us
  transfers between devices with their start and end apart: 1, of which 1 were waited for; matrix products, arithmetic and copies ran while one was open for 0% of the time, Pallas kernels for 0%

commit v1 on v0

v1 whole, which is shorter than its diff:
```python
import jax
import jax.numpy as jnp
from jax import lax
from jax.sharding import PartitionSpec as P

X = 4
Z = 4
DESIGN_MAX = 6.0
WEIGHT_MAX = 0.25
F16_TOP = 32768.0

X_GROUPS = [[z * X + x for x in range(X)] for z in range(Z)]
Z_GROUPS = [[z * X + x for z in range(Z)] for x in range(X)]


def per_device(design, weights, probes, barrier):
    samples, feats = design.shape
    columns = probes.shape[1]
    n_feat = lax.axis_size("feat")
    feat = lax.axis_index("feat")
    owned = feats // (X * Z)
    half = samples // 2
    rows = half // n_feat
    probes_t = probes.T

    partial = jnp.dot(design, probes, preferred_element_type=jnp.float32)
    packed = jnp.concatenate([partial[:half], partial[half:]], axis=1).reshape(n_feat, rows, 2 * columns)
    mass = jnp.sum(jnp.abs(probes_t.astype(jnp.float32)), axis=1)
    mass = jnp.concatenate([mass, mass])
    sent = jnp.concatenate([packed, jnp.broadcast_to(mass, (n_feat, 1, 2 * columns))], axis=1)
    got = lax.all_to_all(sent, "feat", 0, 0).sum(0)
    projected, total_mass = got[:rows], got[rows, :columns]

    low = lax.dynamic_slice_in_dim(weights, feat * rows, rows, 0)
    high = lax.dynamic_slice_in_dim(weights, half + feat * rows, rows, 0)
    factor = jnp.concatenate(
        [jnp.broadcast_to(low[:, None], (rows, columns)), jnp.broadcast_to(high[:, None], (rows, columns))], axis=1
    )
    own = (factor * projected).astype(jnp.bfloat16)
    gathered = lax.all_to_all(jnp.broadcast_to(own, (n_feat, rows, 2 * columns)), "feat", 0, 0)
    gathered = gathered.reshape(half, 2 * columns)
    scaled = jnp.concatenate([gathered[:, :columns], gathered[:, columns:]], axis=0)

    bound = (X * samples) * DESIGN_MAX * WEIGHT_MAX * DESIGN_MAX * jnp.maximum(total_mass, 1e-30)[:, None]
    down, up = F16_TOP / bound, bound / F16_TOP
    hessian = lax.dot_general(scaled, design, (((0,), (0,)), ((), ())), preferred_element_type=jnp.float32)
    sent = (hessian * down).astype(jnp.float16).reshape(columns, Z, X, owned).transpose(2, 1, 0, 3)
    got = lax.all_to_all(sent, "samp", 0, 0, axis_index_groups=X_GROUPS)
    sent = got.astype(jnp.float32).sum(0).astype(jnp.float16)
    got = lax.all_to_all(sent, "samp", 0, 0, axis_index_groups=Z_GROUPS)
    summed = got.astype(jnp.float32).sum(0) * up

    own_probes = lax.dynamic_slice_in_dim(probes_t, lax.axis_index("samp") * owned, owned, 1)
    return (summed + barrier[None, :] * own_probes.astype(jnp.float32)).T


def solution(mesh):
    placed = (P("samp", "feat"), P("samp"), P("feat", None), P(("feat", "samp")))
    return jax.shard_map(
        per_device, mesh=mesh, in_specs=placed, out_specs=P(("feat", "samp"), None), check_vma=False
    )
```

time: 287 us -> 94 us (0.33)
  the two profiles are of different devices: /device:TPU:1 before, /device:TPU:2 now
where the time goes in v1:
time: 94 us; the launch traced here: 93.6 us
  waiting for transfers between devices  34.4 us (37%)
  starting transfers between devices  25.2 us (27%)
  blocking collectives  18.4 us (20%)
  local copies, waits for them, and re-layouts  6.19 us (7%)
  other arithmetic  5.17 us (6%)
  matrix products  4.08 us (4%)
    all_to_all x1, waiting for transfers between devices, per_device(): got = lax.all_to_all(sent, 'samp', 0, 0, axis_index_groups=Z_GROUPS)  18.7 us
    all_to_all x1, blocking collectives, per_device(): got = lax.all_to_all(sent, 'samp', 0, 0, axis_index_groups=X_GROUPS)  18.4 us
    all_to_all x1, starting transfers between devices, per_device(): got = lax.all_to_all(sent, 'samp', 0, 0, axis_index_groups=Z_GROUPS)  12.4 us
    all_to_all x1, starting transfers between devices, per_device(): got = lax.all_to_all(sent, 'feat', 0, 0).sum(0)  8.92 us
    all_to_all x1, waiting for transfers between devices, per_device(): got = lax.all_to_all(sent, 'feat', 0, 0).sum(0)  7.91 us
    all_to_all x1, waiting for transfers between devices, per_device(): lax.all_to_all(jnp.broadcast_to(own, (n_feat, rows, 2 * columns)), 'feat'...  7.81 us
    reshape x2, local copies, waits for them, and re-layouts, per_device(): (hessian * down).astype(jnp.float16).reshape(columns, Z, X, owned)  4.61 us
    all_to_all x1, starting transfers between devices, per_device(): lax.all_to_all(jnp.broadcast_to(own, (n_feat, rows, 2 * columns)), 'feat'...  3.85 us
  transfers between devices with their start and end apart: 3, of which 3 were waited for; matrix products, arithmetic and copies ran while one was open for 0% of the time, Pallas kernels for 0%

profile of v1, /device:TPU:2, one launch (start us, length us, event | category | flops | bytes accessed | tf_op | source)
XLA Modules:
  0.0 93.6 jit_solution(9760907448168712285)
XLA Ops:
  0.0 0.0 copy-start
  0.0 1.7 %abs_reduce_fusion = f32[64]{0:T(128)S(1)} fusion(bf16[8192,64]{0,1:T(8,128)(2,1)} %param.6), kind=kLoop, calls=%fused_computation.3 | loop fusion | flops 1572800 | bytes 1048832 | tf_op jit(solution)/shard_map/reduce_sum | solution.py:28
  1.7 0.0 copy-start.2
  1.7 0.1 pad_maximum_fusion.2
  1.8 0.4 copy-done
  2.2 2.3 %fusion.9 = f32[192,64]{0,1:T(8,128)S(1)} fusion(bf16[192,8192]{1,0:T(8,128)(2,1)S(1)} %copy-done, bf16[8192,64]{0,1:T(8,128)(2,1)} %param.6), kind=kOutput, calls=%fused_computation.22 | convolution fusion | flops 201326592 | bytes 4243456 | tf_op jit(solution)/shard_map/dot_general | solution.py:26
  4.6 0.1 fusion.6
  4.6 0.1 copy.13
  4.8 0.7 pad_maximum_fusion.1
  5.4 8.9 %all-to-all-start = ((f32[32,4,128]{2,1,0:T(4,128)}), f32[32,4,128]{2,1,0:T(4,128)S(1)}, u32[]{:S(2)}, u32[]{:S(2)}) async-start(f32[32,4,128]{2,1,0:T(4,128)} %pad_maximum_fusion.1), calls=%async_computation | async-start | bytes 131072 | tf_op jit(solution)/shard_map/all_to_all | solution.py:31
  14.4 0.0 copy-done.2
  14.4 0.1 fusion.8
  14.5 7.9 %all-to-all-done = f32[32,4,128]{2,1,0:T(4,128)S(1)} async-done(((f32[32,4,128]{2,1,0:T(4,128)}), f32[32,4,128]{2,1,0:T(4,128)S(1)}, u32[]{:S(2)}, u32[]{:S(2)}) %all-to-all-start) | async-done | bytes 65568 | tf_op jit(solution)/shard_map/all_to_all | solution.py:31
  22.4 0.1 broadcast_in_dim.8
  22.5 0.1 broadcast_in_dim.9
  22.6 0.1 fusion.4
  22.6 0.6 broadcast_in_dim.11
  23.3 3.9 %all-to-all-start.1 = ((bf16[32,3,128]{2,1,0:T(4,128)(2,1)}), bf16[32,3,128]{2,1,0:T(4,128)(2,1)S(1)}, u32[]{:S(2)}, u32[]{:S(2)}) async-start(bf16[32,3,128]{2,1,0:T(4,128)(2,1)} %broadcast_in_dim.11), calls=%async_computation.1 | async-start | bytes 65536 | tf_op jit(solution)/shard_map/all_to_all | solution.py:40
  27.1 7.8 %all-to-all-done.1 = bf16[32,3,128]{2,1,0:T(4,128)(2,1)S(1)} async-done(((bf16[32,3,128]{2,1,0:T(4,128)(2,1)}), bf16[32,3,128]{2,1,0:T(4,128)(2,1)S(1)}, u32[]{:S(2)}, u32[]{:S(2)}) %all-to-all-start.1) | async-done | bytes 24608 | tf_op jit(solution)/shard_map/all_to_all | solution.py:40
  35.0 0.1 fusion.7
  35.1 1.7 %fusion = f16[64,8192]{1,0:T(8,128)(2,1)} fusion(bf16[192,8192]{1,0:T(8,128)(2,1)S(1)} %copy-done, f32[64]{0:T(128)S(1)} %get-tuple-element.10, bf16[96,64]{1,0:T(8,128)(2,1)S(1)} %get-tuple-element.8, bf16[96,64]{1,0:T(8,128)(2,1)S(1)} %get-tuple-element.7), kind=kOutput, calls=%fused_computation.1 | convolution fusion | flops 202424320 | bytes 4219136 | tf_op jit(solution)/shard_map/dot_general | solution.py:46
  36.8 2.8 %reshape.36 = f16[64,4,4,512]{3,2,1,0:T(4,128)(2,1)} reshape(f16[64,8192]{1,0:T(8,128)(2,1)} %fusion) | data formatting | bytes 2097152 | tf_op jit(solution)/shard_map/reshape | solution.py:47
  39.6 1.8 %copy.22 = f16[64,4,4,512]{3,1,0,2:T(4,128)(2,1)S(1)} copy(f16[64,4,4,512]{3,2,1,0:T(4,128)(2,1)} %reshape.36) | data formatting | bytes 2097152 | tf_op jit(solution)/shard_map/reshape | solution.py:47
  41.4 0.0 copy-start.1
  41.4 18.4 %all_to_all.20 = f16[4,4,64,512]{3,1,2,0:T(4,128)(2,1)S(1)} all-to-all(f16[4,4,64,512]{3,1,2,0:T(4,128)(2,1)S(1)} %bitcast.12), channel_id=1, replica_groups={{0,32,64,96},{128,160,192,224},{256,288,320,352},{384,416,448,480},{1,3..., dimensions={0} | all-to-all | bytes 2097152 | tf_op jit(solution)/shard_map/all_to_all | solution.py:48
  59.8 0.3 convert_reduce_fusion
  60.1 0.7 convert_element_type.30
  60.8 12.4 %all-to-all-start.3 = ((f16[4,64,512]{2,1,0:T(8,128)(2,1)}), f16[4,64,512]{2,1,0:T(8,128)(2,1)S(1)}, u32[]{:S(2)}, u32[]{:S(2)}) async-start(f16[4,64,512]{2,1,0:T(8,128)(2,1)} %convert_element_type.30), calls=%async_computation.3 | async-start | bytes 524288 | tf_op jit(solution)/shard_map/all_to_all | solution.py:50
  73.2 18.7 %all-to-all-done.3 = f16[4,64,512]{2,1,0:T(8,128)(2,1)S(1)} async-done(((f16[4,64,512]{2,1,0:T(8,128)(2,1)}), f16[4,64,512]{2,1,0:T(8,128)(2,1)S(1)}, u32[]{:S(2)}, u32[]{:S(2)}) %all-to-all-start.3) | async-done | bytes 262176 | tf_op jit(solution)/shard_map/all_to_all | solution.py:50
  92.0 0.0 copy-done.1
  92.0 1.6 %bitcast_add_fusion = f32[512,64]{0,1:T(8,128)} fusion(f32[64,512]{1,0:T(8,128)S(1)} %convert_reduce_fusion.1, bf16[8192,64]{0,1:T(8,128)(2,1)} %param.6, s32[]{:T(128)S(6)} %select_n.11, f32[512]{0:T(512)S(1)} %copy-done.1, f32[64]{0:T(128)S(1)} %get-tuple-element.9), kind=kLoop, calls=%fused_computation.6 | loop fusion | flops 131072 | bytes 329988 | tf_op jit(solution)/shard_map/add | solution.py:54
  (7 shorter events, 0.2 us)
Async XLA Ops:
  0.0 2.2 %copy-start = (bf16[192,8192]{1,0:T(8,128)(2,1)S(1)}, bf16[192,8192]{1,0:T(8,128)(2,1)}, u32[]{:S(2)}) copy-start(bf16[192,8192]{1,0:T(8,128)(2,1)} %param.4) | copy-start | bytes 9437188
  1.7 12.7 %copy-start.2 = (f32[192]{0:T(256)S(1)}, f32[192]{0:T(256)}, u32[]{:S(2)}) copy-start(f32[192]{0:T(256)} %param.5) | copy-start | bytes 2308
  5.4 16.9 %all-to-all-start = ((f32[32,4,128]{2,1,0:T(4,128)}), f32[32,4,128]{2,1,0:T(4,128)S(1)}, u32[]{:S(2)}, u32[]{:S(2)}) async-start(f32[32,4,128]{2,1,0:T(4,128)} %pad_maximum_fusion.1), calls=%async_computation | async-start | bytes 131072 | tf_op jit(solution)/shard_map/all_to_all | solution.py:31
  23.3 11.7 %all-to-all-start.1 = ((bf16[32,3,128]{2,1,0:T(4,128)(2,1)}), bf16[32,3,128]{2,1,0:T(4,128)(2,1)S(1)}, u32[]{:S(2)}, u32[]{:S(2)}) async-start(bf16[32,3,128]{2,1,0:T(4,128)(2,1)} %broadcast_in_dim.11), calls=%async_computation.1 | async-start | bytes 65536 | tf_op jit(solution)/shard_map/all_to_all | solution.py:40
  41.4 50.5 %copy-start.1 = (f32[512]{0:T(512)S(1)}, f32[512]{0:T(512)}, u32[]{:S(2)}) copy-start(f32[512]{0:T(512)} %param.7) | copy-start | bytes 6148
  60.8 31.1 %all-to-all-start.3 = ((f16[4,64,512]{2,1,0:T(8,128)(2,1)}), f16[4,64,512]{2,1,0:T(8,128)(2,1)S(1)}, u32[]{:S(2)}, u32[]{:S(2)}) async-start(f16[4,64,512]{2,1,0:T(8,128)(2,1)} %convert_element_type.30), calls=%async_computation.3 | async-start | bytes 524288 | tf_op jit(solution)/shard_map/all_to_all | solution.py:50

commit v2 on v1

v2 whole, which is shorter than its diff:
```python
import jax
import jax.numpy as jnp
from jax import lax
from jax.experimental import pallas as pl
from jax.experimental.pallas import tpu as pltpu
from jax.sharding import PartitionSpec as P

X = 4
Z = 4
DESIGN_MAX = 6.0
WEIGHT_MAX = 0.25
F16_TOP = 32768.0

X_GROUPS = [[z * X + x for x in range(X)] for z in range(Z)]
Z_GROUPS = [[z * X + x for z in range(Z)] for x in range(X)]


def project_kernel(design_ref, probes_ref, packed_ref, mass_ref, total, mass):
    step = pl.program_id(0)
    probes = probes_ref[...]
    contract = (((1,), (1,)), ((), ()))
    part = lax.dot_general(design_ref[...], probes, contract, preferred_element_type=jnp.float32)
    ones = jnp.ones((8, probes.shape[1]), jnp.bfloat16)
    part_mass = lax.dot_general(ones, jnp.abs(probes), contract, preferred_element_type=jnp.float32)

    @pl.when(step == 0)
    def _():
        total[...] = part
        mass[...] = part_mass

    @pl.when(step > 0)
    def _():
        total[...] += part
        mass[...] += part_mass

    @pl.when(step == pl.num_programs(0) - 1)
    def _():
        half = total.shape[0] // 2
        packed_ref[...] = jnp.concatenate([total[:half], total[half:]], axis=1)
        mass_ref[...] = jnp.concatenate([mass[...], mass[...]], axis=1)


def project(design, probes_t):
    samples, feats = design.shape
    columns = probes_t.shape[0]
    block = 2048
    return pl.pallas_call(
        project_kernel,
        grid=(feats // block,),
        in_specs=[
            pl.BlockSpec((samples, block), lambda i: (0, i)),
            pl.BlockSpec((columns, block), lambda i: (0, i)),
        ],
        out_specs=[
            pl.BlockSpec((samples // 2, 2 * columns), lambda i: (0, 0)),
            pl.BlockSpec((8, 2 * columns), lambda i: (0, 0)),
        ],
        out_shape=[
            jax.ShapeDtypeStruct((samples // 2, 2 * columns), jnp.float32),
            jax.ShapeDtypeStruct((8, 2 * columns), jnp.float32),
        ],
        scratch_shapes=[
            pltpu.VMEM((samples, columns), jnp.float32),
            pltpu.VMEM((8, columns), jnp.float32),
        ],
        compiler_params=pltpu.CompilerParams(vmem_limit_bytes=60 * 1024 * 1024),
        cost_estimate=pl.CostEstimate(
            flops=2 * samples * feats * columns, bytes_accessed=2 * feats * (samples + columns), transcendentals=0
        ),
    )(design, probes_t)


def sketch_kernel(gathered_ref, mass_ref, design_ref, out_ref):
    columns = out_ref.shape[2]
    owned = out_ref.shape[3]
    gathered = gathered_ref[...]
    scaled = jnp.concatenate([gathered[:, :columns], gathered[:, columns:]], axis=0)
    row = jnp.broadcast_to(mass_ref[...][:1, :columns], (columns, columns))
    same = lax.broadcasted_iota(jnp.int32, row.shape, 0) == lax.broadcasted_iota(jnp.int32, row.shape, 1)
    mass = jnp.sum(jnp.where(same, row, 0.0), axis=1, keepdims=True)
    down = F16_TOP / size_bound(mass, scaled.shape[0])
    for z in range(Z):
        for x in range(X):
            at = (z * X + x) * owned
            part = lax.dot_general(
                scaled, design_ref[:, at : at + owned], (((0,), (0,)), ((), ())), preferred_element_type=jnp.float32
            )
            out_ref[x, z] = part * down


def sketch_parts(gathered, mass, design):
    samples, feats = design.shape
    columns = gathered.shape[1] // 2
    return pl.pallas_call(
        sketch_kernel,
        out_shape=jax.ShapeDtypeStruct((X, Z, columns, feats // (X * Z)), jnp.float32),
        in_specs=[pl.BlockSpec(memory_space=pltpu.VMEM)] * 3,
        out_specs=pl.BlockSpec(memory_space=pltpu.VMEM),
        compiler_params=pltpu.CompilerParams(vmem_limit_bytes=16 * 1024 * 1024),
        cost_estimate=pl.CostEstimate(
            flops=2 * samples * feats * columns, bytes_accessed=2 * feats * (samples + 2 * columns), transcendentals=0
        ),
    )(gathered, mass, design)


def size_bound(mass, samples):
    return (X * samples * DESIGN_MAX * WEIGHT_MAX * DESIGN_MAX) * jnp.maximum(mass, 1e-30)


def per_device(design, weights, probes, barrier):
    samples, feats = design.shape
    columns = probes.shape[1]
    n_feat = lax.axis_size("feat")
    feat = lax.axis_index("feat")
    owned = feats // (X * Z)
    half = samples // 2
    rows = half // n_feat
    probes_t = probes.T

    packed, mass = project(design, probes_t)
    packed = packed.reshape(n_feat, rows, 2 * columns)
    sent = jnp.concatenate([packed, jnp.broadcast_to(mass[:1], (n_feat, 1, 2 * columns))], axis=1)
    got = lax.all_to_all(sent, "feat", 0, 0).sum(0)
    projected, total_mass = got[:rows], got[rows:]

    low = lax.dynamic_slice_in_dim(weights, feat * rows, rows, 0)
    high = lax.dynamic_slice_in_dim(weights, half + feat * rows, rows, 0)
    factor = jnp.concatenate(
        [jnp.broadcast_to(low[:, None], (rows, columns)), jnp.broadcast_to(high[:, None], (rows, columns))], axis=1
    )
    own = (factor * projected).astype(jnp.bfloat16)
    gathered = lax.all_to_all(jnp.broadcast_to(own, (n_feat, rows, 2 * columns)), "feat", 0, 0)
    gathered = gathered.reshape(half, 2 * columns)

    up = size_bound(total_mass[0, :columns], samples)[:, None] / F16_TOP
    own_probes = lax.dynamic_slice_in_dim(probes_t, lax.axis_index("samp") * owned, owned, 1)
    diagonal = barrier[None, :] * own_probes.astype(jnp.float32)
    up = jnp.broadcast_to(up, diagonal.shape)
    gathered, diagonal, up = lax.optimization_barrier((gathered, diagonal, up))

    sent = sketch_parts(gathered, total_mass, design).astype(jnp.float16)
    got = lax.all_to_all(sent, "samp", 0, 0, axis_index_groups=X_GROUPS)
    sent = got.astype(jnp.float32).sum(0).astype(jnp.float16)
    got = lax.all_to_all(sent, "samp", 0, 0, axis_index_groups=Z_GROUPS)
    return (got.astype(jnp.float32).sum(0) * up + diagonal).T


def solution(mesh):
    placed = (P("samp", "feat"), P("samp"), P("feat", None), P(("feat", "samp")))
    return jax.shard_map(
        per_device, mesh=mesh, in_specs=placed, out_specs=P(("feat", "samp"), None), check_vma=False
    )
```

time: 94 us -> 89.7 us (0.954)
  the two profiles are of different devices: /device:TPU:2 before, /device:TPU:32 now
where the time goes in v2:
time: 89.7 us; the launch traced here: 89.3 us
  blocking collectives  51.9 us (58%)
  starting transfers between devices  14.1 us (16%)
  waiting for transfers between devices  12.4 us (14%)
  Pallas kernels  5.44 us (6%)
  other arithmetic  2.85 us (3%)
  local copies, waits for them, and re-layouts  2.46 us (3%)
    all_to_all x1, blocking collectives, per_device(): got = lax.all_to_all(sent, 'samp', 0, 0, axis_index_groups=Z_GROUPS)  32.7 us
    all_to_all x1, blocking collectives, per_device(): got = lax.all_to_all(sent, 'samp', 0, 0, axis_index_groups=X_GROUPS)  19.2 us
    all_to_all x1, starting transfers between devices, per_device(): got = lax.all_to_all(sent, 'feat', 0, 0).sum(0)  8.98 us
    all_to_all x1, waiting for transfers between devices, per_device(): lax.all_to_all(jnp.broadcast_to(own, (n_feat, rows, 2 * columns)), 'feat'...  6.62 us
    all_to_all x1, waiting for transfers between devices, per_device(): got = lax.all_to_all(sent, 'feat', 0, 0).sum(0)  5.8 us
    all_to_all x1, starting transfers between devices, per_device(): lax.all_to_all(jnp.broadcast_to(own, (n_feat, rows, 2 * columns)), 'feat'...  5.11 us
    pallas_call x1, Pallas kernels, project(): pl.pallas_call(project_kernel, grid=(feats // block,), in_specs=[pl.Block...  4.63 us
  transfers between devices with their start and end apart: 2, of which 2 were waited for; matrix products, arithmetic and copies ran while one was open for 1% of the time, Pallas kernels for 0%

profile of v2, /device:TPU:32, one launch (start us, length us, event | category | flops | bytes accessed | tf_op | source)
XLA Modules:
  0.0 89.3 jit_solution(4556366430369489482)
XLA Ops:
  0.0 0.0 copy-start.2
  0.0 0.0 copy-start.1
  0.0 0.0 copy-start
  0.0 4.6 %shard_map.46 = (f32[96,128]{1,0:T(8,128)}, f32[8,128]{1,0:T(8,128)}) custom-call(bf16[192,8192]{1,0:T(8,128)(2,1)} %design_ref.3, bf16[64,8192]{1,0:T(8,128)(2,1)} %bitcast.9), custom_call_target="tpu_custom_call" | custom-call | flops 201326592 | bytes 4194304 | tf_op jit(solution)/shard_map/pallas_call | solution.py:47
  4.6 0.7 slice_bitcast_fusion
  5.3 0.8 reshape.21
  6.2 0.7 pad_maximum_fusion
  6.8 9.0 %all-to-all-start = ((f32[32,4,128]{2,1,0:T(4,128)}), f32[32,4,128]{2,1,0:T(4,128)S(1)}, u32[]{:S(2)}, u32[]{:S(2)}) async-start(f32[32,4,128]{2,1,0:T(4,128)} %pad_maximum_fusion), calls=%async_computation | async-start | bytes 131072 | tf_op jit(solution)/shard_map/all_to_all | solution.py:123
  15.8 0.0 copy-done.2
  15.8 0.1 fusion.1
  15.9 0.0 copy-done.1
  15.9 0.9 multiply_bitcast_fusion
  16.8 5.8 %all-to-all-done = f32[32,4,128]{2,1,0:T(4,128)S(1)} async-done(((f32[32,4,128]{2,1,0:T(4,128)}), f32[32,4,128]{2,1,0:T(4,128)S(1)}, u32[]{:S(2)}, u32[]{:S(2)}) %all-to-all-start) | async-done | bytes 65568 | tf_op jit(solution)/shard_map/all_to_all | solution.py:123
  22.6 0.1 broadcast_in_dim.10
  22.7 0.1 broadcast_in_dim.11
  22.7 0.1 fusion
  22.8 0.6 broadcast_in_dim.13
  23.5 5.1 %all-to-all-start.1 = ((bf16[32,3,128]{2,1,0:T(4,128)(2,1)}), bf16[32,3,128]{2,1,0:T(4,128)(2,1)S(1)}, u32[]{:S(2)}, u32[]{:S(2)}) async-start(bf16[32,3,128]{2,1,0:T(4,128)(2,1)} %broadcast_in_dim.13), calls=%async_computation.1 | async-start | bytes 65536 | tf_op jit(solution)/shard_map/all_to_all | solution.py:132
  28.6 6.6 %all-to-all-done.1 = bf16[32,3,128]{2,1,0:T(4,128)(2,1)S(1)} async-done(((bf16[32,3,128]{2,1,0:T(4,128)(2,1)}), bf16[32,3,128]{2,1,0:T(4,128)(2,1)S(1)}, u32[]{:S(2)}, u32[]{:S(2)}) %all-to-all-start.1) | async-done | bytes 24608 | tf_op jit(solution)/shard_map/all_to_all | solution.py:132
  35.2 0.1 broadcast_in_dim.14
  35.3 0.0 copy-done
  35.3 0.8 shard_map.47
  36.1 0.3 convert_element_type.21
  36.4 19.2 %all_to_all.20 = f16[4,4,64,512]{3,2,1,0:T(8,128)(2,1)S(1)} all-to-all(f16[4,4,64,512]{3,2,1,0:T(8,128)(2,1)S(1)} %convert_element_type.21), channel_id=1, replica_groups={{0,32,64,96},{128,160,192,224},{256,288,320,352},{384,416,448,480},{1,3..., dimensions={0} | all-to-all | bytes 2097152 | tf_op jit(solution)/shard_map/all_to_all | solution.py:142
  55.6 0.2 convert_reduce_fusion
  55.8 32.7 %all_to_all.21 = f16[4,64,512]{2,1,0:T(8,128)(2,1)S(1)} all-to-all(f16[4,64,512]{2,1,0:T(8,128)(2,1)S(1)} %convert_element_type.23), channel_id=1, replica_groups={{0,128,256,384},{32,160,288,416},{64,192,320,448},{96,224,352,480},{1,1..., dimensions={0} | all-to-all | bytes 524288 | tf_op jit(solution)/shard_map/all_to_all | solution.py:144
  88.6 0.7 add_bitcast_fusion
  (7 shorter events, 0.2 us)
Async XLA Ops:
  0.0 15.8 %copy-start.2 = (f32[192]{0:T(256)S(1)}, f32[192]{0:T(256)}, u32[]{:S(2)}) copy-start(f32[192]{0:T(256)} %param.5) | copy-start | bytes 2308
  0.0 15.9 %copy-start.1 = (f32[512]{0:T(512)S(1)}, f32[512]{0:T(512)}, u32[]{:S(2)}) copy-start(f32[512]{0:T(512)} %param.7) | copy-start | bytes 6148
  0.0 35.3 %copy-start = (bf16[192,8192]{1,0:T(8,128)(2,1)S(1)}, bf16[192,8192]{1,0:T(8,128)(2,1)}, u32[]{:S(2)}) copy-start(bf16[192,8192]{1,0:T(8,128)(2,1)} %design_ref.3) | copy-start | bytes 9437188
  6.8 15.7 %all-to-all-start = ((f32[32,4,128]{2,1,0:T(4,128)}), f32[32,4,128]{2,1,0:T(4,128)S(1)}, u32[]{:S(2)}, u32[]{:S(2)}) async-start(f32[32,4,128]{2,1,0:T(4,128)} %pad_maximum_fusion), calls=%async_computation | async-start | bytes 131072 | tf_op jit(solution)/shard_map/all_to_all | solution.py:123
  23.5 11.8 %all-to-all-start.1 = ((bf16[32,3,128]{2,1,0:T(4,128)(2,1)}), bf16[32,3,128]{2,1,0:T(4,128)(2,1)S(1)}, u32[]{:S(2)}, u32[]{:S(2)}) async-start(bf16[32,3,128]{2,1,0:T(4,128)(2,1)} %broadcast_in_dim.13), calls=%async_computation.1 | async-start | bytes 65536 | tf_op jit(solution)/shard_map/all_to_all | solution.py:132

commit v3 on v1

v3 whole, which is shorter than its diff:
```python
import jax
import jax.numpy as jnp
from jax import lax
from jax.experimental import pallas as pl
from jax.experimental.pallas import tpu as pltpu
from jax.sharding import PartitionSpec as P

X = 4
Y = 4
Z = 4
CORES = 2
CHUNKS = 8
DESIGN_MAX = 6.0
WEIGHT_MAX = 0.25
F16_TOP = 32768.0

X_GROUPS = [[z * X + x for x in range(X)] for z in range(Z)]
Z_GROUPS = [[z * X + x for z in range(Z)] for x in range(X)]
YC_GROUPS = [[(y * Z + z) * CORES + c for y in range(Y) for c in range(CORES)] for z in range(Z)]
ZLO_GROUPS = [[(y * Z + z) * CORES + c for z in range(Z)] for y in range(Y) for c in range(CORES)]

VMEM = pl.BlockSpec(memory_space=pltpu.VMEM)


def row_of(column):
    n = column.shape[0]
    same = lax.broadcasted_iota(jnp.int32, (n, n), 0) == lax.broadcasted_iota(jnp.int32, (n, n), 1)
    return jnp.sum(jnp.where(same, jnp.broadcast_to(column, (n, n)), 0.0), axis=0, keepdims=True)


def column_of(row):
    n = row.shape[1]
    same = lax.broadcasted_iota(jnp.int32, (n, n), 0) == lax.broadcasted_iota(jnp.int32, (n, n), 1)
    return jnp.sum(jnp.where(same, jnp.broadcast_to(row, (n, n)), 0.0), axis=1, keepdims=True)


def project_kernel(design_ref, probes_ref, out_ref, design_buf, probes_buf, sems):
    width = design_ref.shape[1] // CHUNKS
    copies = []
    for i in range(CHUNKS):
        at = pl.ds(i * width, width)
        pair = [
            pltpu.make_async_copy(probes_ref.at[:, at], probes_buf.at[:, at], sems.at[0, i]),
            pltpu.make_async_copy(design_ref.at[:, at], design_buf.at[:, at], sems.at[1, i]),
        ]
        for copy in pair:
            copy.start()
        copies.append(pair)
    total, mass = 0.0, 0.0
    for i in range(CHUNKS):
        for copy in copies[i]:
            copy.wait()
        design = design_buf[:, i * width : (i + 1) * width]
        probes = probes_buf[:, i * width : (i + 1) * width]
        total += lax.dot_general(design, probes, (((1,), (1,)), ((), ())), preferred_element_type=jnp.float32)
        size = jnp.abs(probes).astype(jnp.float32)
        for j in range(width // 128):
            mass += size[:, j * 128 : (j + 1) * 128]
    half = total.shape[0] // 2
    packed = jnp.concatenate([total[:half], total[half:]], axis=1)
    row = row_of(jnp.sum(mass, axis=1, keepdims=True))
    row = jnp.broadcast_to(jnp.concatenate([row, row], axis=1), (8, packed.shape[1]))
    for i in range(out_ref.shape[0]):
        out_ref[i, :half] = packed
        out_ref[i, half:] = row


def project(design, probes_t):
    samples, feats = design.shape
    columns = probes_t.shape[0]
    return pl.pallas_call(
        project_kernel,
        in_specs=[pl.BlockSpec(memory_space=pl.ANY)] * 2,
        out_specs=VMEM,
        out_shape=jax.ShapeDtypeStruct((Y * CORES, samples // 2 + 8, 2 * columns), jnp.float32),
        scratch_shapes=[
            pltpu.VMEM((samples, feats), jnp.bfloat16),
            pltpu.VMEM((columns, feats), jnp.bfloat16),
            pltpu.SemaphoreType.DMA((2, CHUNKS)),
        ],
        compiler_params=pltpu.CompilerParams(vmem_limit_bytes=60 * 1024 * 1024),
        cost_estimate=pl.CostEstimate(
            flops=2 * samples * feats * columns, bytes_accessed=2 * feats * (samples + columns), transcendentals=0
        ),
    )(design, probes_t)


def resum_kernel(in_ref, out_ref):
    total = in_ref[0]
    for i in range(1, in_ref.shape[0]):
        total += in_ref[i]
    for i in range(out_ref.shape[0]):
        out_ref[i] = total


def resum(parts):
    shape = (Z,) + parts.shape[1:]
    return pl.pallas_call(
        resum_kernel,
        in_specs=[VMEM],
        out_specs=VMEM,
        out_shape=jax.ShapeDtypeStruct(shape, jnp.float32),
        compiler_params=pltpu.CompilerParams(vmem_limit_bytes=8 * 1024 * 1024),
        cost_estimate=pl.CostEstimate(flops=parts.size, bytes_accessed=6 * parts.size, transcendentals=0),
    )(parts)


def sketch_kernel(parts_ref, factor_ref, design_ref, out_ref, up_ref):
    columns, owned = out_ref.shape[2:]
    half = factor_ref.shape[0]
    total = parts_ref[0]
    for i in range(1, parts_ref.shape[0]):
        total += parts_ref[i]
    scaled = (factor_ref[...] * total[:half]).astype(jnp.bfloat16)
    scaled = jnp.concatenate([scaled[:, :columns], scaled[:, columns:]], axis=0)
    mass = column_of(total[half : half + 1, :columns])
    bound = (X * 2 * half * DESIGN_MAX * WEIGHT_MAX * DESIGN_MAX) * jnp.maximum(mass, 1e-30)
    down = F16_TOP / bound
    up_ref[...] = jnp.broadcast_to(bound / F16_TOP, up_ref.shape)
    for z in range(Z):
        for x in range(X):
            at = (z * X + x) * owned
            part = lax.dot_general(
                scaled, design_ref[:, at : at + owned], (((0,), (0,)), ((), ())), preferred_element_type=jnp.float32
            )
            out_ref[x, z] = part * down


def sketch_parts(parts, factor, design):
    samples, feats = design.shape
    columns = parts.shape[2] // 2
    owned = feats // (X * Z)
    return pl.pallas_call(
        sketch_kernel,
        in_specs=[VMEM] * 3,
        out_specs=[VMEM] * 2,
        out_shape=[
            jax.ShapeDtypeStruct((X, Z, columns, owned), jnp.float32),
            jax.ShapeDtypeStruct((columns, owned), jnp.float32),
        ],
        compiler_params=pltpu.CompilerParams(vmem_limit_bytes=16 * 1024 * 1024),
        cost_estimate=pl.CostEstimate(
            flops=2 * samples * feats * columns, bytes_accessed=2 * feats * (samples + 2 * columns), transcendentals=0
        ),
    )(parts, factor, design)


def per_device(design, weights, probes, barrier):
    samples, feats = design.shape
    columns = probes.shape[1]
    owned = feats // (X * Z)
    half = samples // 2
    probes_t = probes.T

    own_probes = lax.dynamic_slice_in_dim(probes_t, lax.axis_index("samp") * owned, owned, 1)
    diagonal = barrier[None, :] * own_probes.astype(jnp.float32)
    factor = jnp.concatenate([jnp.broadcast_to(w[:, None], (half, columns)) for w in (weights[:half], weights[half:])], axis=1)

    parts = lax.all_to_all(project(design, probes_t), "feat", 0, 0, axis_index_groups=YC_GROUPS)
    parts = lax.all_to_all(resum(parts), "feat", 0, 0, axis_index_groups=ZLO_GROUPS)
    parts, factor, diagonal = lax.optimization_barrier((parts, factor, diagonal))

    sent, up = sketch_parts(parts, factor, design)
    got = lax.all_to_all(sent.astype(jnp.float16), "samp", 0, 0, axis_index_groups=X_GROUPS)
    sent = got.astype(jnp.float32).sum(0).astype(jnp.float16)
    got = lax.all_to_all(sent, "samp", 0, 0, axis_index_groups=Z_GROUPS)
    return (got.astype(jnp.float32).sum(0) * up + diagonal).T


def solution(mesh):
    placed = (P("samp", "feat"), P("samp"), P("feat", None), P(("feat", "samp")))
    return jax.shard_map(
        per_device, mesh=mesh, in_specs=placed, out_specs=P(("feat", "samp"), None), check_vma=False
    )
```

time: 94 us -> 81.3 us (0.86)
  the two profiles are of different devices: /device:TPU:2 before, /device:TPU:32 now
where the time goes in v3:
time: 81.3 us; the launch traced here: 80.9 us
  blocking collectives  59.8 us (74%)
  starting transfers between devices  7.72 us (9%)
  Pallas kernels  5.83 us (7%)
  waiting for transfers between devices  5.09 us (6%)
  other arithmetic  2.15 us (3%)
    all_to_all x1, blocking collectives, per_device(): got = lax.all_to_all(sent, 'samp', 0, 0, axis_index_groups=Z_GROUPS)  29.7 us
    all_to_all x1, blocking collectives, per_device(): lax.all_to_all(sent.astype(jnp.float16), 'samp', 0, 0, axis_index_groups=...  16.3 us
    all_to_all x1, blocking collectives, per_device(): lax.all_to_all(project(design, probes_t), 'feat', 0, 0, axis_index_groups...  13.8 us
    all_to_all x1, starting transfers between devices, per_device(): lax.all_to_all(resum(parts), 'feat', 0, 0, axis_index_groups=ZLO_GROUPS)  7.72 us
    all_to_all x1, waiting for transfers between devices, per_device(): lax.all_to_all(resum(parts), 'feat', 0, 0, axis_index_groups=ZLO_GROUPS)  5.09 us
    pallas_call x1, Pallas kernels, project(): pl.pallas_call(project_kernel, in_specs=[pl.BlockSpec(memory_space=pl.ANY...  4.32 us
  transfers between devices with their start and end apart: 1, of which 1 were waited for; matrix products, arithmetic and copies ran while one was open for 1% of the time, Pallas kernels for 0%

profile of v3, /device:TPU:32, one launch (start us, length us, event | category | flops | bytes accessed | tf_op | source)
XLA Modules:
  0.0 80.9 jit_solution(11409866044316533470)
XLA Ops:
  0.0 0.0 copy-start.2
  0.0 0.0 copy-start
  0.0 4.3 %shard_map.46 = f32[8,104,128]{2,1,0:T(8,128)} custom-call(bf16[192,8192]{1,0:T(8,128)(2,1)} %design_ref.3, bf16[64,8192]{1,0:T(8,128)(2,1)} %bitcast.5), custom_call_target="tpu_custom_call" | custom-call | flops 201326592 | bytes 4194304 | tf_op jit(solution)/shard_map/pallas_call | solution.py:71
  4.3 0.0 copy-start.1
  4.3 13.8 %all_to_all.20.in_ref = f32[8,104,128]{2,1,0:T(8,128)S(1)} all-to-all(f32[8,104,128]{2,1,0:T(8,128)} %shard_map.46), channel_id=1, replica_groups={{0,1,8,9,16,17,24,25},{2,3,10,11,18,19,26,27},{4,5,12,13,20,21,28,29},{..., dimensions={0} | all-to-all | bytes 851968 | tf_op jit(solution)/shard_map/all_to_all | solution.py:159
  18.1 0.7 shard_map.47
  18.8 7.7 %all-to-all-start.1 = ((f32[4,104,128]{2,1,0:T(8,128)}), f32[4,104,128]{2,1,0:T(8,128)S(1)}, u32[]{:S(2)}, u32[]{:S(2)}) async-start(f32[4,104,128]{2,1,0:T(8,128)} %shard_map.47), calls=%async_computation.1 | async-start | bytes 425984 | tf_op jit(solution)/shard_map/all_to_all | solution.py:160
  26.5 0.0 copy-done.2
  26.5 0.1 fusion
  26.6 0.1 broadcast_in_dim.4
  26.7 0.1 broadcast_in_dim.5
  26.8 0.1 pad_maximum_fusion.factor_ref
  26.9 0.0 copy-done.1
  26.9 0.9 %multiply_bitcast_fusion = f32[64,512]{1,0:T(8,128)S(1)} fusion(bf16[8192,64]{0,1:T(8,128)(2,1)} %param.6, s32[]{:T(128)S(6)} %select_n.3, f32[512]{0:T(512)S(1)} %copy-done.1), kind=kLoop, calls=%fused_computation.3 | loop fusion | flops 65536 | bytes 198660 | tf_op jit(solution)/shard_map/mul | solution.py:156
  27.7 5.1 %all-to-all-done.1.parts_ref = f32[4,104,128]{2,1,0:T(8,128)S(1)} async-done(((f32[4,104,128]{2,1,0:T(8,128)}), f32[4,104,128]{2,1,0:T(8,128)S(1)}, u32[]{:S(2)}, u32[]{:S(2)}) %all-to-all-start.1) | async-done | bytes 213024 | tf_op jit(solution)/shard_map/all_to_all | solution.py:160
  32.8 0.0 copy-done
  32.8 0.8 %shard_map.48 = (f32[4,4,64,512]{3,2,1,0:T(8,128)S(1)}, f32[64,512]{1,0:T(8,128)S(1)}) custom-call(f32[4,104,128]{2,1,0:T(8,128)S(1)} %all-to-all-done.1.parts_ref, f32[96,128]{1,0:T(8,128)S(1)} %pad_maximum_fusion.factor_ref, bf16[192,8192]{1,0:T(8,128)(2,1)S(1)} %copy-done), custom_call_target="tpu_custom_call" | custom-call | flops 201326592 | bytes 5242880 | tf_op jit(solution)/shard_map/pallas_call | solution.py:133
  33.6 0.3 convert_element_type.17
  33.9 16.3 %all_to_all.21 = f16[4,4,64,512]{3,2,1,0:T(8,128)(2,1)S(1)} all-to-all(f16[4,4,64,512]{3,2,1,0:T(8,128)(2,1)S(1)} %convert_element_type.17), channel_id=1, replica_groups={{0,32,64,96},{128,160,192,224},{256,288,320,352},{384,416,448,480},{1,3..., dimensions={0} | all-to-all | bytes 2097152 | tf_op jit(solution)/shard_map/all_to_all | solution.py:164
  50.2 0.2 convert_reduce_fusion
  50.4 29.7 %all_to_all.22 = f16[4,64,512]{2,1,0:T(8,128)(2,1)S(1)} all-to-all(f16[4,64,512]{2,1,0:T(8,128)(2,1)S(1)} %convert_element_type.19), channel_id=1, replica_groups={{0,128,256,384},{32,160,288,416},{64,192,320,448},{96,224,352,480},{1,1..., dimensions={0} | all-to-all | bytes 524288 | tf_op jit(solution)/shard_map/all_to_all | solution.py:166
  80.2 0.7 add_bitcast_fusion
  (2 shorter events, 0.1 us)
Async XLA Ops:
  0.0 26.5 %copy-start.2 = (f32[192]{0:T(256)S(1)}, f32[192]{0:T(256)}, u32[]{:S(2)}) copy-start(f32[192]{0:T(256)} %param.5) | copy-start | bytes 2308
  0.0 32.8 %copy-start = (bf16[192,8192]{1,0:T(8,128)(2,1)S(1)}, bf16[192,8192]{1,0:T(8,128)(2,1)}, u32[]{:S(2)}) copy-start(bf16[192,8192]{1,0:T(8,128)(2,1)} %design_ref.3) | copy-start | bytes 9437188
  4.3 22.5 %copy-start.1 = (f32[512]{0:T(512)S(1)}, f32[512]{0:T(512)}, u32[]{:S(2)}) copy-start(f32[512]{0:T(512)} %param.7) | copy-start | bytes 6148
  18.8 14.0 %all-to-all-start.1 = ((f32[4,104,128]{2,1,0:T(8,128)}), f32[4,104,128]{2,1,0:T(8,128)S(1)}, u32[]{:S(2)}, u32[]{:S(2)}) async-start(f32[4,104,128]{2,1,0:T(8,128)} %shard_map.47), calls=%async_computation.1 | async-start | bytes 425984 | tf_op jit(solution)/shard_map/all_to_all | solution.py:160

commit v4 on v3

--- a/solution.py
+++ b/solution.py
@@ -15,7 +15,7 @@
 F16_TOP = 32768.0
 
 X_GROUPS = [[z * X + x for x in range(X)] for z in range(Z)]
-Z_GROUPS = [[z * X + x for z in range(Z)] for x in range(X)]
+FAR_FIRST = (2, 1, 3)
 YC_GROUPS = [[(y * Z + z) * CORES + c for y in range(Y) for c in range(CORES)] for z in range(Z)]
 ZLO_GROUPS = [[(y * Z + z) * CORES + c for z in range(Z)] for y in range(Y) for c in range(CORES)]
 
@@ -105,7 +105,7 @@
     )(parts)
 
 
-def sketch_kernel(parts_ref, factor_ref, design_ref, out_ref, up_ref):
+def sketch_kernel(own_z, parts_ref, factor_ref, design_ref, out_ref, up_ref):
     columns, owned = out_ref.shape[2:]
     half = factor_ref.shape[0]
     total = parts_ref[0]
@@ -123,7 +123,7 @@
             part = lax.dot_general(
                 scaled, design_ref[:, at : at + owned], (((0,), (0,)), ((), ())), preferred_element_type=jnp.float32
             )
-            out_ref[x, z] = part * down
+            out_ref[x, lax.rem(z + Z - own_z[0], Z)] = part * down
 
 
 def sketch_parts(parts, factor, design):
@@ -132,7 +132,7 @@
     owned = feats // (X * Z)
     return pl.pallas_call(
         sketch_kernel,
-        in_specs=[VMEM] * 3,
+        in_specs=[pl.BlockSpec(memory_space=pltpu.SMEM)] + [VMEM] * 3,
         out_specs=[VMEM] * 2,
         out_shape=[
             jax.ShapeDtypeStruct((X, Z, columns, owned), jnp.float32),
@@ -142,7 +142,7 @@
         cost_estimate=pl.CostEstimate(
             flops=2 * samples * feats * columns, bytes_accessed=2 * feats * (samples + 2 * columns), transcendentals=0
         ),
-    )(parts, factor, design)
+    )((lax.axis_index("samp") // X).reshape(1), parts, factor, design)
 
 
 def per_device(design, weights, probes, barrier):
@@ -163,8 +163,11 @@
     sent, up = sketch_parts(parts, factor, design)
     got = lax.all_to_all(sent.astype(jnp.float16), "samp", 0, 0, axis_index_groups=X_GROUPS)
     sent = got.astype(jnp.float32).sum(0).astype(jnp.float16)
-    got = lax.all_to_all(sent, "samp", 0, 0, axis_index_groups=Z_GROUPS)
-    return (got.astype(jnp.float32).sum(0) * up + diagonal).T
+    total = sent[0].astype(jnp.float32)
+    for far in FAR_FIRST:
+        step = [(z * X + x, (z + far) % Z * X + x) for z in range(Z) for x in range(X)]
+        total += lax.ppermute(sent[far], "samp", step).astype(jnp.float32)
+    return (total * up + diagonal).T
 
 
 def solution(mesh):

time: 81.3 us -> 78.3 us (0.963)
  blocking collectives: 59.8 us -> 30.1 us
  starting transfers between devices: 7.72 us -> 30.3 us
  waiting for transfers between devices: 5.09 us -> 9.11 us
    all_to_all x1 -> x0, blocking collectives: 29.7 us -> none  [per_device(): got = lax.all_to_all(sent, 'samp', 0, 0, axis_index_groups=Z_GROUPS)]
    ppermute x0 -> x3, starting transfers between devices: none -> 22.6 us  [per_device(): total += lax.ppermute(sent[far], 'samp', step).astype(jnp.float32)]
    ppermute x0 -> x3, waiting for transfers between devices: none -> 4.03 us  [per_device(): total += lax.ppermute(sent[far], 'samp', step).astype(jnp.float32)]
  transfers between devices with their start and end apart: 1 -> 4, of which waited for: 1 -> 3; matrix products, arithmetic and copies ran while one was open for 1% -> 1% of each run, Pallas kernels for 0% -> 0%
where the time goes in v4:
time: 78.3 us; the launch traced here: 77.9 us
  starting transfers between devices  30.3 us (39%)
  blocking collectives  30.1 us (38%)
  waiting for transfers between devices  9.11 us (12%)
  Pallas kernels  5.15 us (7%)
  other arithmetic  2.14 us (3%)
  local copies, waits for them, and re-layouts  0.94 us (1%)
    ppermute x3, starting transfers between devices, per_device(): total += lax.ppermute(sent[far], 'samp', step).astype(jnp.float32)  22.6 us
    all_to_all x1, blocking collectives, per_device(): lax.all_to_all(sent.astype(jnp.float16), 'samp', 0, 0, axis_index_groups=...  16.3 us
    all_to_all x1, blocking collectives, per_device(): lax.all_to_all(project(design, probes_t), 'feat', 0, 0, axis_index_groups...  13.8 us
    all_to_all x1, starting transfers between devices, per_device(): lax.all_to_all(resum(parts), 'feat', 0, 0, axis_index_groups=ZLO_GROUPS)  7.72 us
    all_to_all x1, waiting for transfers between devices, per_device(): lax.all_to_all(resum(parts), 'feat', 0, 0, axis_index_groups=ZLO_GROUPS)  5.08 us
    pallas_call x1, Pallas kernels, project(): pl.pallas_call(project_kernel, in_specs=[pl.BlockSpec(memory_space=pl.ANY...  4.32 us
    ppermute x3, waiting for transfers between devices, per_device(): total += lax.ppermute(sent[far], 'samp', step).astype(jnp.float32)  4.03 us
  transfers between devices with their start and end apart: 4, of which 3 were waited for; matrix products, arithmetic and copies ran while one was open for 1% of the time, Pallas kernels for 0%

profile of v4, /device:TPU:32, one launch (start us, length us, event | category | flops | bytes accessed | tf_op | source)
XLA Modules:
  0.0 77.9 jit_solution(10950062619582242844)
XLA Ops:
  0.0 0.0 copy-start.3
  0.0 0.0 copy-start
  0.0 4.3 %shard_map.46 = f32[8,104,128]{2,1,0:T(8,128)} custom-call(bf16[192,8192]{1,0:T(8,128)(2,1)} %design_ref.3, bf16[64,8192]{1,0:T(8,128)(2,1)} %bitcast.17), custom_call_target="tpu_custom_call" | custom-call | flops 201326592 | bytes 4194304 | tf_op jit(solution)/shard_map/pallas_call | solution.py:71
  4.3 0.0 copy-start.2
  4.3 13.8 %all_to_all.15.in_ref = f32[8,104,128]{2,1,0:T(8,128)S(1)} all-to-all(f32[8,104,128]{2,1,0:T(8,128)} %shard_map.46), channel_id=1, replica_groups={{0,1,8,9,16,17,24,25},{2,3,10,11,18,19,26,27},{4,5,12,13,20,21,28,29},{..., dimensions={0} | all-to-all | bytes 851968 | tf_op jit(solution)/shard_map/all_to_all | solution.py:159
  18.1 0.0 copy-start.1
  18.2 0.7 copy-done.1
  18.8 7.7 %all-to-all-start.1 = ((f32[4,104,128]{2,1,0:T(8,128)}), f32[4,104,128]{2,1,0:T(8,128)S(1)}, u32[]{:S(2)}, u32[]{:S(2)}) async-start(f32[4,104,128]{2,1,0:T(8,128)} %copy-done.1), calls=%async_computation.1 | async-start | bytes 425984 | tf_op jit(solution)/shard_map/all_to_all | solution.py:160
  26.5 0.0 copy-done.3
  26.5 0.1 fusion.5
  26.6 0.1 broadcast_in_dim.4
  26.7 0.1 broadcast_in_dim.5
  26.8 0.1 pad_maximum_fusion.factor_ref
  26.9 0.0 copy-done.2
  26.9 0.9 %multiply_bitcast_fusion = f32[64,512]{1,0:T(8,128)S(1)} fusion(bf16[8192,64]{0,1:T(8,128)(2,1)} %param.6, s32[]{:T(128)S(6)} %select_n.9, f32[512]{0:T(512)S(1)} %copy-done.2), kind=kLoop, calls=%fused_computation.7 | loop fusion | flops 65536 | bytes 198660 | tf_op jit(solution)/shard_map/mul | solution.py:156
  27.7 5.1 %all-to-all-done.1.parts_ref = f32[4,104,128]{2,1,0:T(8,128)S(1)} async-done(((f32[4,104,128]{2,1,0:T(8,128)}), f32[4,104,128]{2,1,0:T(8,128)S(1)}, u32[]{:S(2)}, u32[]{:S(2)}) %all-to-all-start.1) | async-done | bytes 213024 | tf_op jit(solution)/shard_map/all_to_all | solution.py:160
  32.8 0.0 copy-done
  32.8 0.8 %shard_map.48 = (f32[4,4,64,512]{3,2,1,0:T(8,128)S(1)}, f32[64,512]{1,0:T(8,128)S(1)}) custom-call(s32[1]{0:T(128)} %bitcast.own_z, f32[4,104,128]{2,1,0:T(8,128)S(1)} %all-to-all-done.1.parts_ref, f32[96,128]{1,0:T(8,128)S(1)} %pad_maximum_fusion.factor_ref, bf16[192,8192]{1,0:T(8,128)(2,1)S(1)} %copy-done), custom_call_target="tpu_custom_call" | custom-call | flops 201326592 | bytes 5242880 | tf_op jit(solution)/shard_map/pallas_call | solution.py:133
  33.6 0.3 convert_element_type.29
  33.9 16.3 %all_to_all.16 = f16[4,4,64,512]{3,2,1,0:T(8,128)(2,1)S(1)} all-to-all(f16[4,4,64,512]{3,2,1,0:T(8,128)(2,1)S(1)} %convert_element_type.29), channel_id=1, replica_groups={{0,32,64,96},{128,160,192,224},{256,288,320,352},{384,416,448,480},{1,3..., dimensions={0} | all-to-all | bytes 2097152 | tf_op jit(solution)/shard_map/all_to_all | solution.py:164
  50.2 0.2 convert_reduce_fusion
  50.5 12.8 %collective-permute-start = (f16[64,512]{1,0:T(8,128)(2,1)S(1)}, f16[64,512]{1,0:T(8,128)(2,1)S(1)}, u32[]{:S(2)}, u32[]{:S(2)}) collective-permute-start(f16[64,512]{1,0:T(8,128)(2,1)S(1)} %get-tuple-element.15), channel_id=1, source_target_pairs={{0,256},{32,288},{64,320},{96,352},{128,384},{160,416},{192,448},{... | collective-permute-start | bytes 196616 | tf_op jit(solution)/shard_map/ppermute | solution.py:169
  63.4 2.7 %collective-permute-start.2 = (f16[64,512]{1,0:T(8,128)(2,1)S(1)}, f16[64,512]{1,0:T(8,128)(2,1)S(1)}, u32[]{:S(2)}, u32[]{:S(2)}) collective-permute-start(f16[64,512]{1,0:T(8,128)(2,1)S(1)} %get-tuple-element.16), channel_id=1, source_target_pairs={{0,384},{32,416},{64,448},{96,480},{128,0},{160,32},{192,64},{224,... | collective-permute-start | bytes 196616 | tf_op jit(solution)/shard_map/ppermute | solution.py:169
  66.0 7.1 %collective-permute-start.1 = (f16[64,512]{1,0:T(8,128)(2,1)S(1)}, f16[64,512]{1,0:T(8,128)(2,1)S(1)}, u32[]{:S(2)}, u32[]{:S(2)}) collective-permute-start(f16[64,512]{1,0:T(8,128)(2,1)S(1)} %get-tuple-element.17), channel_id=1, source_target_pairs={{0,128},{32,160},{64,192},{96,224},{128,256},{160,288},{192,320},{... | collective-permute-start | bytes 196616 | tf_op jit(solution)/shard_map/ppermute | solution.py:169
  73.1 0.0 collective-permute-done
  73.1 1.5 %collective-permute-done.2 = f16[64,512]{1,0:T(8,128)(2,1)S(1)} collective-permute-done((f16[64,512]{1,0:T(8,128)(2,1)S(1)}, f16[64,512]{1,0:T(8,128)(2,1)S(1)}, u32[]{:S(2)}, u32[]{:S(2)}) %collective-permute-start.2) | collective-permute-done | bytes 65568 | tf_op jit(solution)/shard_map/ppermute | solution.py:169
  74.6 2.5 %collective-permute-done.1 = f16[64,512]{1,0:T(8,128)(2,1)S(1)} collective-permute-done((f16[64,512]{1,0:T(8,128)(2,1)S(1)}, f16[64,512]{1,0:T(8,128)(2,1)S(1)}, u32[]{:S(2)}, u32[]{:S(2)}) %collective-permute-start.1) | collective-permute-done | bytes 65568 | tf_op jit(solution)/shard_map/ppermute | solution.py:169
  77.2 0.7 fusion.4
  (3 shorter events, 0.1 us)
Async XLA Ops:
  0.0 26.5 %copy-start.3 = (f32[192]{0:T(256)S(1)}, f32[192]{0:T(256)}, u32[]{:S(2)}) copy-start(f32[192]{0:T(256)} %param.5) | copy-start | bytes 2308
  0.0 32.8 %copy-start = (bf16[192,8192]{1,0:T(8,128)(2,1)S(1)}, bf16[192,8192]{1,0:T(8,128)(2,1)}, u32[]{:S(2)}) copy-start(bf16[192,8192]{1,0:T(8,128)(2,1)} %design_ref.3) | copy-start | bytes 9437188
  4.3 22.5 %copy-start.2 = (f32[512]{0:T(512)S(1)}, f32[512]{0:T(512)}, u32[]{:S(2)}) copy-start(f32[512]{0:T(512)} %param.7) | copy-start | bytes 6148
  18.1 0.7 copy-start.1
  18.8 14.0 %all-to-all-start.1 = ((f32[4,104,128]{2,1,0:T(8,128)}), f32[4,104,128]{2,1,0:T(8,128)S(1)}, u32[]{:S(2)}, u32[]{:S(2)}) async-start(f32[4,104,128]{2,1,0:T(8,128)} %copy-done.1), calls=%async_computation.1 | async-start | bytes 425984 | tf_op jit(solution)/shard_map/all_to_all | solution.py:160
  50.5 22.6 %collective-permute-start = (f16[64,512]{1,0:T(8,128)(2,1)S(1)}, f16[64,512]{1,0:T(8,128)(2,1)S(1)}, u32[]{:S(2)}, u32[]{:S(2)}) collective-permute-start(f16[64,512]{1,0:T(8,128)(2,1)S(1)} %get-tuple-element.15), channel_id=1, source_target_pairs={{0,256},{32,288},{64,320},{96,352},{128,384},{160,416},{192,448},{... | collective-permute-start | bytes 196616 | tf_op jit(solution)/shard_map/ppermute | solution.py:169
  63.4 11.3 %collective-permute-start.2 = (f16[64,512]{1,0:T(8,128)(2,1)S(1)}, f16[64,512]{1,0:T(8,128)(2,1)S(1)}, u32[]{:S(2)}, u32[]{:S(2)}) collective-permute-start(f16[64,512]{1,0:T(8,128)(2,1)S(1)} %get-tuple-element.16), channel_id=1, source_target_pairs={{0,384},{32,416},{64,448},{96,480},{128,0},{160,32},{192,64},{224,... | collective-permute-start | bytes 196616 | tf_op jit(solution)/shard_map/ppermute | solution.py:169
  66.0 11.1 %collective-permute-start.1 = (f16[64,512]{1,0:T(8,128)(2,1)S(1)}, f16[64,512]{1,0:T(8,128)(2,1)S(1)}, u32[]{:S(2)}, u32[]{:S(2)}) collective-permute-start(f16[64,512]{1,0:T(8,128)(2,1)S(1)} %get-tuple-element.17), channel_id=1, source_target_pairs={{0,128},{32,160},{64,192},{96,224},{128,256},{160,288},{192,320},{... | collective-permute-start | bytes 196616 | tf_op jit(solution)/shard_map/ppermute | solution.py:169

commit v5 on v4

v5 whole, which is shorter than its diff:
```python
import jax
import jax.numpy as jnp
from jax import lax
from jax.experimental import pallas as pl
from jax.experimental.pallas import tpu as pltpu
from jax.sharding import PartitionSpec as P

X = 4
Y = 4
Z = 4
CORES = 2
CHUNKS = 2
DESIGN_MAX = 6.0
WEIGHT_MAX = 0.25
F16_TOP = 32768.0

X_GROUPS = [[z * X + x for x in range(X)] for z in range(Z)]
FAR_FIRST = (2, 1, 3)
YC_GROUPS = [[(y * Z + z) * CORES + c for y in range(Y) for c in range(CORES)] for z in range(Z)]
ZLO_GROUPS = [[(y * Z + z) * CORES + c for z in range(Z)] for y in range(Y) for c in range(CORES)]

VMEM = pl.BlockSpec(memory_space=pltpu.VMEM)


def row_of(column):
    n = column.shape[0]
    same = lax.broadcasted_iota(jnp.int32, (n, n), 0) == lax.broadcasted_iota(jnp.int32, (n, n), 1)
    return jnp.sum(jnp.where(same, jnp.broadcast_to(column, (n, n)), 0.0), axis=0, keepdims=True)


def column_of(row):
    n = row.shape[1]
    same = lax.broadcasted_iota(jnp.int32, (n, n), 0) == lax.broadcasted_iota(jnp.int32, (n, n), 1)
    return jnp.sum(jnp.where(same, jnp.broadcast_to(row, (n, n)), 0.0), axis=1, keepdims=True)


def project_kernel(own, barrier_ref, design_ref, probes_ref, out_ref, diagonal_ref, total, mass):
    step = pl.program_id(0)
    width = probes_ref.shape[1]
    half, owned = total.shape[0] // 2, diagonal_ref.shape[1]

    @pl.when(step == 0)
    def _():
        total[...] = jnp.zeros_like(total)
        mass[...] = jnp.zeros_like(mass)

    total[...] += lax.dot_general(
        design_ref[...], probes_ref[...], (((1,), (1,)), ((), ())), preferred_element_type=jnp.float32
    )
    size = jnp.abs(probes_ref[...]).astype(jnp.float32)
    for j in range(width // 128):
        mass[...] += size[:, j * 128 : (j + 1) * 128]

    blocks = width // owned

    @pl.when(step == lax.div(own[0], blocks))
    def _():
        at = pl.multiple_of(lax.rem(own[0], blocks) * owned, owned)
        diagonal_ref[...] = barrier_ref[...] * probes_ref[:, pl.ds(at, owned)].astype(jnp.float32)

    @pl.when(step == pl.num_programs(0) - 1)
    def _():
        packed = jnp.concatenate([total[:half], total[half:]], axis=1)
        row = row_of(jnp.sum(mass[...], axis=1, keepdims=True))
        row = jnp.broadcast_to(jnp.concatenate([row, row], axis=1), (8, packed.shape[1]))
        for i in range(out_ref.shape[0]):
            out_ref[i, :half] = packed
            out_ref[i, half:] = row


def project(own, barrier, design, probes_t):
    samples, feats = design.shape
    columns, owned = probes_t.shape[0], barrier.shape[1]
    half, width = samples // 2, feats // CHUNKS
    return pl.pallas_call(
        project_kernel,
        grid=(CHUNKS,),
        in_specs=[
            pl.BlockSpec(memory_space=pltpu.SMEM),
            pl.BlockSpec((1, owned), lambda i: (0, 0)),
            pl.BlockSpec((samples, width), lambda i: (0, i)),
            pl.BlockSpec((columns, width), lambda i: (0, i)),
        ],
        out_specs=[
            pl.BlockSpec((Y * CORES, half + 8, 2 * columns), lambda i: (0, 0, 0)),
            pl.BlockSpec((columns, owned), lambda i: (0, 0)),
        ],
        out_shape=[
            jax.ShapeDtypeStruct((Y * CORES, half + 8, 2 * columns), jnp.float32),
            jax.ShapeDtypeStruct((columns, owned), jnp.float32),
        ],
        scratch_shapes=[pltpu.VMEM((samples, columns), jnp.float32), pltpu.VMEM((columns, 128), jnp.float32)],
        compiler_params=pltpu.CompilerParams(vmem_limit_bytes=60 * 1024 * 1024),
        cost_estimate=pl.CostEstimate(
            flops=2 * samples * feats * columns, bytes_accessed=2 * feats * (samples + columns), transcendentals=0
        ),
    )(own, barrier, design, probes_t)


def resum_kernel(in_ref, out_ref):
    total = in_ref[0]
    for i in range(1, in_ref.shape[0]):
        total += in_ref[i]
    for i in range(out_ref.shape[0]):
        out_ref[i] = total


def resum(parts):
    shape = (Z,) + parts.shape[1:]
    return pl.pallas_call(
        resum_kernel,
        in_specs=[VMEM],
        out_specs=VMEM,
        out_shape=jax.ShapeDtypeStruct(shape, jnp.float32),
        compiler_params=pltpu.CompilerParams(vmem_limit_bytes=8 * 1024 * 1024),
        cost_estimate=pl.CostEstimate(flops=parts.size, bytes_accessed=6 * parts.size, transcendentals=0),
    )(parts)


def sketch_kernel(own, weights_ref, parts_ref, design_ref, out_ref, up_ref):
    columns, owned = out_ref.shape[2:]
    half = design_ref.shape[0] // 2
    own_z = lax.div(own[0], X)
    total = parts_ref[0]
    for i in range(1, parts_ref.shape[0]):
        total += parts_ref[i]
    projected = jnp.concatenate([total[:half, :columns], total[:half, columns:]], axis=0)
    scaled = (column_of(weights_ref[...]) * projected).astype(jnp.bfloat16)
    mass = column_of(total[half : half + 1, :columns])
    bound = (X * 2 * half * DESIGN_MAX * WEIGHT_MAX * DESIGN_MAX) * jnp.maximum(mass, 1e-30)
    down = F16_TOP / bound
    up_ref[...] = jnp.broadcast_to(bound / F16_TOP, up_ref.shape)
    for z in range(Z):
        for x in range(X):
            at = (z * X + x) * owned
            part = lax.dot_general(
                scaled, design_ref[:, at : at + owned], (((0,), (0,)), ((), ())), preferred_element_type=jnp.float32
            )
            out_ref[x, lax.rem(z + Z - own_z, Z)] = part * down


def sketch_parts(own, weights, parts, design):
    samples, feats = design.shape
    columns = parts.shape[2] // 2
    owned = feats // (X * Z)
    return pl.pallas_call(
        sketch_kernel,
        in_specs=[pl.BlockSpec(memory_space=pltpu.SMEM)] + [VMEM] * 3,
        out_specs=[VMEM] * 2,
        out_shape=[
            jax.ShapeDtypeStruct((X, Z, columns, owned), jnp.float32),
            jax.ShapeDtypeStruct((columns, owned), jnp.float32),
        ],
        compiler_params=pltpu.CompilerParams(vmem_limit_bytes=16 * 1024 * 1024),
        cost_estimate=pl.CostEstimate(
            flops=2 * samples * feats * columns, bytes_accessed=2 * feats * (samples + 2 * columns), transcendentals=0
        ),
    )(own, weights, parts, design)


def per_device(design, weights, probes, barrier):
    own, weights, barrier = lax.axis_index("samp").reshape(1), weights[None, :], barrier[None, :]
    own, weights, barrier = lax.optimization_barrier((own, weights, barrier))

    parts, diagonal = project(own, barrier, design, probes.T)
    parts = lax.all_to_all(parts, "feat", 0, 0, axis_index_groups=YC_GROUPS)
    parts = lax.all_to_all(resum(parts), "feat", 0, 0, axis_index_groups=ZLO_GROUPS)

    sent, up = sketch_parts(own, weights, parts, design)
    got = lax.all_to_all(sent.astype(jnp.float16), "samp", 0, 0, axis_index_groups=X_GROUPS)
    sent = got.astype(jnp.float32).sum(0).astype(jnp.float16)
    total = sent[0].astype(jnp.float32)
    for far in FAR_FIRST:
        step = [(z * X + x, (z + far) % Z * X + x) for z in range(Z) for x in range(X)]
        total += lax.ppermute(sent[far], "samp", step).astype(jnp.float32)
    return (total * up + diagonal).T


def solution(mesh):
    placed = (P("samp", "feat"), P("samp"), P("feat", None), P(("feat", "samp")))
    return jax.shard_map(
        per_device, mesh=mesh, in_specs=placed, out_specs=P(("feat", "samp"), None), check_vma=False
    )
```

time: 78.3 us -> 77.5 us (0.990)
  the two profiles are of different devices: /device:TPU:32 before, /device:TPU:96 now
where the time goes in v5:
time: 77.5 us; the launch traced here: 77.2 us
  blocking collectives  42.9 us (55%)
  starting transfers between devices  22.8 us (29%)
  waiting for transfers between devices  5.45 us (7%)
  Pallas kernels  4.77 us (6%)
  other arithmetic  1.2 us (2%)
    ppermute x3, starting transfers between devices, per_device(): total += lax.ppermute(sent[far], 'samp', step).astype(jnp.float32)  22.8 us
    all_to_all x1, blocking collectives, per_device(): lax.all_to_all(sent.astype(jnp.float16), 'samp', 0, 0, axis_index_groups=...  17.8 us
    all_to_all x1, blocking collectives, per_device(): parts = lax.all_to_all(parts, 'feat', 0, 0, axis_index_groups=YC_GROUPS)  13.8 us
    all_to_all x1, blocking collectives, per_device(): lax.all_to_all(resum(parts), 'feat', 0, 0, axis_index_groups=ZLO_GROUPS)  11.3 us
    ppermute x3, waiting for transfers between devices, per_device(): total += lax.ppermute(sent[far], 'samp', step).astype(jnp.float32)  5.45 us
    pallas_call x1, Pallas kernels, project(): pl.pallas_call(project_kernel, grid=(CHUNKS,), in_specs=[pl.BlockSpec(mem...  3.87 us
  transfers between devices with their start and end apart: 3, of which 2 were waited for; matrix products, arithmetic and copies ran while one was open for 0% of the time, Pallas kernels for 0%

profile of v5, /device:TPU:96, one launch (start us, length us, event | category | flops | bytes accessed | tf_op | source)
XLA Modules:
  0.0 77.2 jit_solution(15935621652628555783)
XLA Ops:
  0.0 0.0 copy-start
  0.0 0.0 copy-start.1
  0.0 3.9 %shard_map.46 = (f32[8,104,128]{2,1,0:T(8,128)}, f32[64,512]{1,0:T(8,128)}) custom-call(s32[1]{0:T(128)} %bitcast.own, f32[1,512]{1,0:T(1,128)} %bitcast.19, bf16[192,8192]{1,0:T(8,128)(2,1)} %design_ref.3, bf16[64,8192]{1,0:T(8,128)(2,1)} %bitcast.18), custom_call_target="tpu_custom_call" | custom-call | flops 201326592 | bytes 4194304 | tf_op jit(solution)/shard_map/pallas_call | solution.py:75
  3.9 13.8 %all_to_all.15.in_ref = f32[8,104,128]{2,1,0:T(8,128)S(1)} all-to-all(f32[8,104,128]{2,1,0:T(8,128)} %get-tuple-element.15), channel_id=1, replica_groups={{0,1,8,9,16,17,24,25},{2,3,10,11,18,19,26,27},{4,5,12,13,20,21,28,29},{..., dimensions={0} | all-to-all | bytes 851968 | tf_op jit(solution)/shard_map/all_to_all | solution.py:166
  17.7 11.3 %all_to_all.16.parts_ref = f32[4,104,128]{2,1,0:T(8,128)S(1)} all-to-all(f32[4,104,128]{2,1,0:T(8,128)S(1)} %shard_map.47), channel_id=1, replica_groups={{0,2,4,6},{1,3,5,7},{8,10,12,14},{9,11,13,15},{16,18,20,22},{17,19,21,2..., dimensions={0} | all-to-all | bytes 425984 | tf_op jit(solution)/shard_map/all_to_all | solution.py:167
  29.0 0.0 copy-done
  29.0 0.0 copy-done.1
  29.0 0.9 %shard_map.48 = (f32[4,4,64,512]{3,2,1,0:T(8,128)S(1)}, f32[64,512]{1,0:T(8,128)S(1)}) custom-call(s32[1]{0:T(128)} %bitcast.own, f32[1,192]{1,0:T(1,128)S(1)} %bitcast.17, f32[4,104,128]{2,1,0:T(8,128)S(1)} %all_to_all.16.parts_ref, bf16[192,8192]{1,0:T(8,128)(2,1)S(1)} %copy-done), custom_call_target="tpu_custom_call" | custom-call | flops 201326592 | bytes 5242880 | tf_op jit(solution)/shard_map/pallas_call | solution.py:146
  29.9 0.3 convert_element_type.24
  30.2 0.0 copy-start.2
  30.2 17.8 %all_to_all.17 = f16[4,4,64,512]{3,2,1,0:T(8,128)(2,1)S(1)} all-to-all(f16[4,4,64,512]{3,2,1,0:T(8,128)(2,1)S(1)} %convert_element_type.24), channel_id=1, replica_groups={{0,32,64,96},{128,160,192,224},{256,288,320,352},{384,416,448,480},{1,3..., dimensions={0} | all-to-all | bytes 2097152 | tf_op jit(solution)/shard_map/all_to_all | solution.py:170
  47.9 0.2 convert_reduce_fusion
  48.2 13.0 %collective-permute-start = (f16[64,512]{1,0:T(8,128)(2,1)S(1)}, f16[64,512]{1,0:T(8,128)(2,1)S(1)}, u32[]{:S(2)}, u32[]{:S(2)}) collective-permute-start(f16[64,512]{1,0:T(8,128)(2,1)S(1)} %get-tuple-element.19), channel_id=1, source_target_pairs={{0,256},{32,288},{64,320},{96,352},{128,384},{160,416},{192,448},{... | collective-permute-start | bytes 196616 | tf_op jit(solution)/shard_map/ppermute | solution.py:175
  61.3 3.3 %collective-permute-start.2 = (f16[64,512]{1,0:T(8,128)(2,1)S(1)}, f16[64,512]{1,0:T(8,128)(2,1)S(1)}, u32[]{:S(2)}, u32[]{:S(2)}) collective-permute-start(f16[64,512]{1,0:T(8,128)(2,1)S(1)} %get-tuple-element.20), channel_id=1, source_target_pairs={{0,384},{32,416},{64,448},{96,480},{128,0},{160,32},{192,64},{224,... | collective-permute-start | bytes 196616 | tf_op jit(solution)/shard_map/ppermute | solution.py:175
  64.6 6.4 %collective-permute-start.1 = (f16[64,512]{1,0:T(8,128)(2,1)S(1)}, f16[64,512]{1,0:T(8,128)(2,1)S(1)}, u32[]{:S(2)}, u32[]{:S(2)}) collective-permute-start(f16[64,512]{1,0:T(8,128)(2,1)S(1)} %get-tuple-element.21), channel_id=1, source_target_pairs={{0,128},{32,160},{64,192},{96,224},{128,256},{160,288},{192,320},{... | collective-permute-start | bytes 196616 | tf_op jit(solution)/shard_map/ppermute | solution.py:175
  71.0 0.0 collective-permute-done
  71.0 1.6 %collective-permute-done.2 = f16[64,512]{1,0:T(8,128)(2,1)S(1)} collective-permute-done((f16[64,512]{1,0:T(8,128)(2,1)S(1)}, f16[64,512]{1,0:T(8,128)(2,1)S(1)}, u32[]{:S(2)}, u32[]{:S(2)}) %collective-permute-start.2) | collective-permute-done | bytes 65568 | tf_op jit(solution)/shard_map/ppermute | solution.py:175
  72.6 3.8 %collective-permute-done.1 = f16[64,512]{1,0:T(8,128)(2,1)S(1)} collective-permute-done((f16[64,512]{1,0:T(8,128)(2,1)S(1)}, f16[64,512]{1,0:T(8,128)(2,1)S(1)}, u32[]{:S(2)}, u32[]{:S(2)}) %collective-permute-start.1) | collective-permute-done | bytes 65568 | tf_op jit(solution)/shard_map/ppermute | solution.py:175
  76.5 0.0 copy-done.2
  76.5 0.7 fusion.4
  (3 shorter events, 0.1 us)
Async XLA Ops:
  0.0 29.0 %copy-start = (bf16[192,8192]{1,0:T(8,128)(2,1)S(1)}, bf16[192,8192]{1,0:T(8,128)(2,1)}, u32[]{:S(2)}) copy-start(bf16[192,8192]{1,0:T(8,128)(2,1)} %design_ref.3) | copy-start | bytes 9437188
  0.0 29.0 %copy-start.1 = (f32[192]{0:T(256)S(1)}, f32[192]{0:T(256)}, u32[]{:S(2)}) copy-start(f32[192]{0:T(256)} %param.5) | copy-start | bytes 2308
  30.2 46.3 %copy-start.2 = (f32[64,512]{1,0:T(8,128)S(1)}, f32[64,512]{1,0:T(8,128)}, u32[]{:S(2)}) copy-start(f32[64,512]{1,0:T(8,128)} %get-tuple-element.18) | copy-start | bytes 393220
  48.2 22.8 %collective-permute-start = (f16[64,512]{1,0:T(8,128)(2,1)S(1)}, f16[64,512]{1,0:T(8,128)(2,1)S(1)}, u32[]{:S(2)}, u32[]{:S(2)}) collective-permute-start(f16[64,512]{1,0:T(8,128)(2,1)S(1)} %get-tuple-element.19), channel_id=1, source_target_pairs={{0,256},{32,288},{64,320},{96,352},{128,384},{160,416},{192,448},{... | collective-permute-start | bytes 196616 | tf_op jit(solution)/shard_map/ppermute | solution.py:175
  61.3 11.4 %collective-permute-start.2 = (f16[64,512]{1,0:T(8,128)(2,1)S(1)}, f16[64,512]{1,0:T(8,128)(2,1)S(1)}, u32[]{:S(2)}, u32[]{:S(2)}) collective-permute-start(f16[64,512]{1,0:T(8,128)(2,1)S(1)} %get-tuple-element.20), channel_id=1, source_target_pairs={{0,384},{32,416},{64,448},{96,480},{128,0},{160,32},{192,64},{224,... | collective-permute-start | bytes 196616 | tf_op jit(solution)/shard_map/ppermute | solution.py:175
  64.6 11.9 %collective-permute-start.1 = (f16[64,512]{1,0:T(8,128)(2,1)S(1)}, f16[64,512]{1,0:T(8,128)(2,1)S(1)}, u32[]{:S(2)}, u32[]{:S(2)}) collective-permute-start(f16[64,512]{1,0:T(8,128)(2,1)S(1)} %get-tuple-element.21), channel_id=1, source_target_pairs={{0,128},{32,160},{64,192},{96,224},{128,256},{160,288},{192,320},{... | collective-permute-start | bytes 196616 | tf_op jit(solution)/shard_map/ppermute | solution.py:175

commit v6 on v5

--- a/solution.py
+++ b/solution.py
@@ -16,7 +16,7 @@
 
 X_GROUPS = [[z * X + x for x in range(X)] for z in range(Z)]
 FAR_FIRST = (2, 1, 3)
-YC_GROUPS = [[(y * Z + z) * CORES + c for y in range(Y) for c in range(CORES)] for z in range(Z)]
+Y_GROUPS = [[(y * Z + z) * CORES + c for y in range(Y)] for z in range(Z) for c in range(CORES)]
 ZLO_GROUPS = [[(y * Z + z) * CORES + c for z in range(Z)] for y in range(Y) for c in range(CORES)]
 
 VMEM = pl.BlockSpec(memory_space=pltpu.VMEM)
@@ -63,9 +63,8 @@
         packed = jnp.concatenate([total[:half], total[half:]], axis=1)
         row = row_of(jnp.sum(mass[...], axis=1, keepdims=True))
         row = jnp.broadcast_to(jnp.concatenate([row, row], axis=1), (8, packed.shape[1]))
-        for i in range(out_ref.shape[0]):
-            out_ref[i, :half] = packed
-            out_ref[i, half:] = row
+        out_ref[:half] = packed
+        out_ref[half:] = row
 
 
 def project(own, barrier, design, probes_t):
@@ -82,11 +81,11 @@
             pl.BlockSpec((columns, width), lambda i: (0, i)),
         ],
         out_specs=[
-            pl.BlockSpec((Y * CORES, half + 8, 2 * columns), lambda i: (0, 0, 0)),
+            pl.BlockSpec((half + 8, 2 * columns), lambda i: (0, 0)),
             pl.BlockSpec((columns, owned), lambda i: (0, 0)),
         ],
         out_shape=[
-            jax.ShapeDtypeStruct((Y * CORES, half + 8, 2 * columns), jnp.float32),
+            jax.ShapeDtypeStruct((half + 8, 2 * columns), jnp.float32),
             jax.ShapeDtypeStruct((columns, owned), jnp.float32),
         ],
         scratch_shapes=[pltpu.VMEM((samples, columns), jnp.float32), pltpu.VMEM((columns, 128), jnp.float32)],
@@ -97,24 +96,26 @@
     )(own, barrier, design, probes_t)
 
 
-def resum_kernel(in_ref, out_ref):
-    total = in_ref[0]
-    for i in range(1, in_ref.shape[0]):
-        total += in_ref[i]
+def resum_kernel(*refs):
+    out_ref = refs[-1]
+    terms = [ref[i] for ref in refs[:-1] for i in range(ref.shape[0])]
+    total = terms[0]
+    for term in terms[1:]:
+        total += term
     for i in range(out_ref.shape[0]):
         out_ref[i] = total
 
 
-def resum(parts):
-    shape = (Z,) + parts.shape[1:]
+def resum(copies, *parts):
+    size = sum(part.size for part in parts)
     return pl.pallas_call(
         resum_kernel,
-        in_specs=[VMEM],
+        in_specs=[VMEM] * len(parts),
         out_specs=VMEM,
-        out_shape=jax.ShapeDtypeStruct(shape, jnp.float32),
+        out_shape=jax.ShapeDtypeStruct((copies,) + parts[0].shape[1:], jnp.float32),
         compiler_params=pltpu.CompilerParams(vmem_limit_bytes=8 * 1024 * 1024),
-        cost_estimate=pl.CostEstimate(flops=parts.size, bytes_accessed=6 * parts.size, transcendentals=0),
-    )(parts)
+        cost_estimate=pl.CostEstimate(flops=size, bytes_accessed=6 * size, transcendentals=0),
+    )(*parts)
 
 
 def sketch_kernel(own, weights_ref, parts_ref, design_ref, out_ref, up_ref):
@@ -163,8 +164,10 @@
     own, weights, barrier = lax.optimization_barrier((own, weights, barrier))
 
     parts, diagonal = project(own, barrier, design, probes.T)
-    parts = lax.all_to_all(parts, "feat", 0, 0, axis_index_groups=YC_GROUPS)
-    parts = lax.all_to_all(resum(parts), "feat", 0, 0, axis_index_groups=ZLO_GROUPS)
+    parts = parts[None]
+    other = lax.ppermute(parts, "feat", [(i, i ^ 1) for i in range(Y * Z * CORES)])
+    parts = lax.all_to_all(jnp.broadcast_to(parts + other, (Y, *parts.shape[1:])), "feat", 0, 0, axis_index_groups=Y_GROUPS)
+    parts = lax.all_to_all(resum(Z, parts), "feat", 0, 0, axis_index_groups=ZLO_GROUPS)
 
     sent, up = sketch_parts(own, weights, parts, design)
     got = lax.all_to_all(sent.astype(jnp.float16), "samp", 0, 0, axis_index_groups=X_GROUPS)

time: 77.5 us -> 77.2 us (level)
  the two profiles are of different devices: /device:TPU:96 before, /device:TPU:32 now
where the time goes in v6:
time: 77.2 us; the launch traced here: 76.9 us
  blocking collectives  39.2 us (51%)
  starting transfers between devices  24.7 us (32%)
  waiting for transfers between devices  6.17 us (8%)
  Pallas kernels  4.64 us (6%)
  other arithmetic  2.02 us (3%)
    ppermute x3, starting transfers between devices, per_device(): total += lax.ppermute(sent[far], 'samp', step).astype(jnp.float32)  22.8 us
    all_to_all x1, blocking collectives, per_device(): lax.all_to_all(sent.astype(jnp.float16), 'samp', 0, 0, axis_index_groups=...  16.2 us
    all_to_all x1, blocking collectives, per_device(): lax.all_to_all(resum(Z, parts), 'feat', 0, 0, axis_index_groups=ZLO_GROUPS)  12.3 us
    all_to_all x1, blocking collectives, per_device(): lax.all_to_all(jnp.broadcast_to(parts + other, (Y, *parts.shape[1:])), 'f...  10.7 us
    ppermute x3, waiting for transfers between devices, per_device(): total += lax.ppermute(sent[far], 'samp', step).astype(jnp.float32)  4.75 us
    pallas_call x1, Pallas kernels, project(): pl.pallas_call(project_kernel, grid=(CHUNKS,), in_specs=[pl.BlockSpec(mem...  3.75 us
    ppermute x1, starting transfers between devices, per_device(): lax.ppermute(parts, 'feat', [(i, i ^ 1) for i in range(Y * Z * CORES)])  1.91 us
  transfers between devices with their start and end apart: 4, of which 3 were waited for; matrix products, arithmetic and copies ran while one was open for 0% of the time, Pallas kernels for 0%

profile of v6, /device:TPU:32, one launch (start us, length us, event | category | flops | bytes accessed | tf_op | source)
XLA Modules:
  0.0 76.9 jit_solution(7263212259562317884)
XLA Ops:
  0.0 0.0 copy-start
  0.0 0.0 copy-start.1
  0.0 3.7 %shard_map.46 = (f32[104,128]{1,0:T(8,128)}, f32[64,512]{1,0:T(8,128)}) custom-call(s32[1]{0:T(128)} %bitcast.own, f32[1,512]{1,0:T(1,128)} %bitcast.24, bf16[192,8192]{1,0:T(8,128)(2,1)} %design_ref.3, bf16[64,8192]{1,0:T(8,128)(2,1)} %bitcast.22), custom_call_target="tpu_custom_call" | custom-call | flops 201326592 | bytes 4194304 | tf_op jit(solution)/shard_map/pallas_call | solution.py:74
  3.8 1.9 %collective-permute-start = (f32[1,104,128]{2,1,0:T(8,128)}, f32[1,104,128]{2,1,0:T(8,128)S(1)}, u32[]{:S(2)}, u32[]{:S(2)}) collective-permute-start(f32[1,104,128]{2,1,0:T(8,128)} %bitcast.23), channel_id=1, source_target_pairs={{0,1},{1,0},{2,3},{3,2},{4,5},{5,4},{6,7},{7,6},{8,9},{9,8},{10,11... | collective-permute-start | bytes 159752 | tf_op jit(solution)/shard_map/ppermute | solution.py:168
  5.7 1.4 %collective-permute-done = f32[1,104,128]{2,1,0:T(8,128)S(1)} collective-permute-done((f32[1,104,128]{2,1,0:T(8,128)}, f32[1,104,128]{2,1,0:T(8,128)S(1)}, u32[]{:S(2)}, u32[]{:S(2)}) %collective-permute-start) | collective-permute-done | bytes 53280 | tf_op jit(solution)/shard_map/ppermute | solution.py:168
  7.1 0.8 %add_bitcast_fusion = f32[104,128]{1,0:T(8,128)S(1)} fusion(f32[1,104,128]{2,1,0:T(8,128)S(1)} %collective-permute-done, f32[104,128]{1,0:T(8,128)} %get-tuple-element.15), kind=kLoop, calls=%fused_computation.11 | loop fusion | flops 13312 | bytes 159744 | tf_op jit(solution)/shard_map/broadcast_in_dim | solution.py:169
  7.9 10.7 %all_to_all.15.refs_0_ = f32[4,104,128]{2,1,0:T(8,128)S(1)} all-to-all(f32[4,104,128]{2,1,0:T(8,128)S(1)} %broadcast_in_dim.20), channel_id=1, replica_groups={{0,8,16,24},{1,9,17,25},{2,10,18,26},{3,11,19,27},{4,12,20,28},{5,13,21..., dimensions={0} | all-to-all | bytes 425984 | tf_op jit(solution)/shard_map/all_to_all | solution.py:169
  18.7 12.3 %all_to_all.16.parts_ref = f32[4,104,128]{2,1,0:T(8,128)S(1)} all-to-all(f32[4,104,128]{2,1,0:T(8,128)S(1)} %shard_map.47), channel_id=1, replica_groups={{0,2,4,6},{1,3,5,7},{8,10,12,14},{9,11,13,15},{16,18,20,22},{17,19,21,2..., dimensions={0} | all-to-all | bytes 425984 | tf_op jit(solution)/shard_map/all_to_all | solution.py:170
  30.9 0.0 copy-done
  30.9 0.0 copy-done.1
  30.9 0.9 %shard_map.48 = (f32[4,4,64,512]{3,2,1,0:T(8,128)S(1)}, f32[64,512]{1,0:T(8,128)S(1)}) custom-call(s32[1]{0:T(128)} %bitcast.own, f32[1,192]{1,0:T(1,128)S(1)} %bitcast.21, f32[4,104,128]{2,1,0:T(8,128)S(1)} %all_to_all.16.parts_ref, bf16[192,8192]{1,0:T(8,128)(2,1)S(1)} %copy-done), custom_call_target="tpu_custom_call" | custom-call | flops 201326592 | bytes 5242880 | tf_op jit(solution)/shard_map/pallas_call | solution.py:147
  31.8 0.3 convert_element_type.24
  32.1 0.0 copy-start.2
  32.1 16.2 %all_to_all.17 = f16[4,4,64,512]{3,2,1,0:T(8,128)(2,1)S(1)} all-to-all(f16[4,4,64,512]{3,2,1,0:T(8,128)(2,1)S(1)} %convert_element_type.24), channel_id=1, replica_groups={{0,32,64,96},{128,160,192,224},{256,288,320,352},{384,416,448,480},{1,3..., dimensions={0} | all-to-all | bytes 2097152 | tf_op jit(solution)/shard_map/all_to_all | solution.py:173
  48.3 0.2 convert_reduce_fusion
  48.6 13.0 %collective-permute-start.1 = (f16[64,512]{1,0:T(8,128)(2,1)S(1)}, f16[64,512]{1,0:T(8,128)(2,1)S(1)}, u32[]{:S(2)}, u32[]{:S(2)}) collective-permute-start(f16[64,512]{1,0:T(8,128)(2,1)S(1)} %get-tuple-element.19), channel_id=1, source_target_pairs={{0,256},{32,288},{64,320},{96,352},{128,384},{160,416},{192,448},{... | collective-permute-start | bytes 196616 | tf_op jit(solution)/shard_map/ppermute | solution.py:178
  61.6 3.3 %collective-permute-start.3 = (f16[64,512]{1,0:T(8,128)(2,1)S(1)}, f16[64,512]{1,0:T(8,128)(2,1)S(1)}, u32[]{:S(2)}, u32[]{:S(2)}) collective-permute-start(f16[64,512]{1,0:T(8,128)(2,1)S(1)} %get-tuple-element.20), channel_id=1, source_target_pairs={{0,384},{32,416},{64,448},{96,480},{128,0},{160,32},{192,64},{224,... | collective-permute-start | bytes 196616 | tf_op jit(solution)/shard_map/ppermute | solution.py:178
  65.0 6.4 %collective-permute-start.2 = (f16[64,512]{1,0:T(8,128)(2,1)S(1)}, f16[64,512]{1,0:T(8,128)(2,1)S(1)}, u32[]{:S(2)}, u32[]{:S(2)}) collective-permute-start(f16[64,512]{1,0:T(8,128)(2,1)S(1)} %get-tuple-element.21), channel_id=1, source_target_pairs={{0,128},{32,160},{64,192},{96,224},{128,256},{160,288},{192,320},{... | collective-permute-start | bytes 196616 | tf_op jit(solution)/shard_map/ppermute | solution.py:178
  71.4 0.0 collective-permute-done.1
  71.4 1.6 %collective-permute-done.3 = f16[64,512]{1,0:T(8,128)(2,1)S(1)} collective-permute-done((f16[64,512]{1,0:T(8,128)(2,1)S(1)}, f16[64,512]{1,0:T(8,128)(2,1)S(1)}, u32[]{:S(2)}, u32[]{:S(2)}) %collective-permute-start.3) | collective-permute-done | bytes 65568 | tf_op jit(solution)/shard_map/ppermute | solution.py:178
  73.1 3.1 %collective-permute-done.2 = f16[64,512]{1,0:T(8,128)(2,1)S(1)} collective-permute-done((f16[64,512]{1,0:T(8,128)(2,1)S(1)}, f16[64,512]{1,0:T(8,128)(2,1)S(1)}, u32[]{:S(2)}, u32[]{:S(2)}) %collective-permute-start.2) | collective-permute-done | bytes 65568 | tf_op jit(solution)/shard_map/ppermute | solution.py:178
  76.2 0.0 copy-done.2
  76.2 0.7 fusion.4
  (4 shorter events, 0.1 us)
Async XLA Ops:
  0.0 30.9 %copy-start = (bf16[192,8192]{1,0:T(8,128)(2,1)S(1)}, bf16[192,8192]{1,0:T(8,128)(2,1)}, u32[]{:S(2)}) copy-start(bf16[192,8192]{1,0:T(8,128)(2,1)} %design_ref.3) | copy-start | bytes 9437188
  0.0 30.9 %copy-start.1 = (f32[192]{0:T(256)S(1)}, f32[192]{0:T(256)}, u32[]{:S(2)}) copy-start(f32[192]{0:T(256)} %param.5) | copy-start | bytes 2308
  3.8 3.3 %collective-permute-start = (f32[1,104,128]{2,1,0:T(8,128)}, f32[1,104,128]{2,1,0:T(8,128)S(1)}, u32[]{:S(2)}, u32[]{:S(2)}) collective-permute-start(f32[1,104,128]{2,1,0:T(8,128)} %bitcast.23), channel_id=1, source_target_pairs={{0,1},{1,0},{2,3},{3,2},{4,5},{5,4},{6,7},{7,6},{8,9},{9,8},{10,11... | collective-permute-start | bytes 159752 | tf_op jit(solution)/shard_map/ppermute | solution.py:168
  32.1 44.1 %copy-start.2 = (f32[64,512]{1,0:T(8,128)S(1)}, f32[64,512]{1,0:T(8,128)}, u32[]{:S(2)}) copy-start(f32[64,512]{1,0:T(8,128)} %get-tuple-element.18) | copy-start | bytes 393220
  48.6 22.8 %collective-permute-start.1 = (f16[64,512]{1,0:T(8,128)(2,1)S(1)}, f16[64,512]{1,0:T(8,128)(2,1)S(1)}, u32[]{:S(2)}, u32[]{:S(2)}) collective-permute-start(f16[64,512]{1,0:T(8,128)(2,1)S(1)} %get-tuple-element.19), channel_id=1, source_target_pairs={{0,256},{32,288},{64,320},{96,352},{128,384},{160,416},{192,448},{... | collective-permute-start | bytes 196616 | tf_op jit(solution)/shard_map/ppermute | solution.py:178
  61.6 11.4 %collective-permute-start.3 = (f16[64,512]{1,0:T(8,128)(2,1)S(1)}, f16[64,512]{1,0:T(8,128)(2,1)S(1)}, u32[]{:S(2)}, u32[]{:S(2)}) collective-permute-start(f16[64,512]{1,0:T(8,128)(2,1)S(1)} %get-tuple-element.20), channel_id=1, source_target_pairs={{0,384},{32,416},{64,448},{96,480},{128,0},{160,32},{192,64},{224,... | collective-permute-start | bytes 196616 | tf_op jit(solution)/shard_map/ppermute | solution.py:178
  65.0 11.2 %collective-permute-start.2 = (f16[64,512]{1,0:T(8,128)(2,1)S(1)}, f16[64,512]{1,0:T(8,128)(2,1)S(1)}, u32[]{:S(2)}, u32[]{:S(2)}) collective-permute-start(f16[64,512]{1,0:T(8,128)(2,1)S(1)} %get-tuple-element.21), channel_id=1, source_target_pairs={{0,128},{32,160},{64,192},{96,224},{128,256},{160,288},{192,320},{... | collective-permute-start | bytes 196616 | tf_op jit(solution)/shard_map/ppermute | solution.py:178

commit v7 on v6

--- a/solution.py
+++ b/solution.py
@@ -14,7 +14,8 @@
 WEIGHT_MAX = 0.25
 F16_TOP = 32768.0
 
-X_GROUPS = [[z * X + x for x in range(X)] for z in range(Z)]
+X_ORDER = (0, 2, 1, 3)
+X_GROUPS = [[z * X + x for x in X_ORDER] for z in range(Z)]
 FAR_FIRST = (2, 1, 3)
 Y_GROUPS = [[(y * Z + z) * CORES + c for y in range(Y)] for z in range(Z) for c in range(CORES)]
 ZLO_GROUPS = [[(y * Z + z) * CORES + c for z in range(Z)] for y in range(Y) for c in range(CORES)]
@@ -137,7 +138,7 @@
             part = lax.dot_general(
                 scaled, design_ref[:, at : at + owned], (((0,), (0,)), ((), ())), preferred_element_type=jnp.float32
             )
-            out_ref[x, lax.rem(z + Z - own_z, Z)] = part * down
+            out_ref[X_ORDER.index(x), lax.rem(z + Z - own_z, Z)] = part * down
 
 
 def sketch_parts(own, weights, parts, design):

time: 77.2 us -> 76.9 us (level)
  no operation moved by 1% of the time
where the time goes in v7:
time: 76.9 us; the launch traced here: 76.6 us
  blocking collectives  38.9 us (51%)
  starting transfers between devices  24.7 us (32%)
  waiting for transfers between devices  6.17 us (8%)
  Pallas kernels  4.64 us (6%)
  other arithmetic  2.02 us (3%)
    ppermute x3, starting transfers between devices, per_device(): total += lax.ppermute(sent[far], 'samp', step).astype(jnp.float32)  22.8 us
    all_to_all x1, blocking collectives, per_device(): lax.all_to_all(sent.astype(jnp.float16), 'samp', 0, 0, axis_index_groups=...  15.9 us
    all_to_all x1, blocking collectives, per_device(): lax.all_to_all(resum(Z, parts), 'feat', 0, 0, axis_index_groups=ZLO_GROUPS)  12.3 us
    all_to_all x1, blocking collectives, per_device(): lax.all_to_all(jnp.broadcast_to(parts + other, (Y, *parts.shape[1:])), 'f...  10.7 us
    ppermute x3, waiting for transfers between devices, per_device(): total += lax.ppermute(sent[far], 'samp', step).astype(jnp.float32)  4.75 us
    pallas_call x1, Pallas kernels, project(): pl.pallas_call(project_kernel, grid=(CHUNKS,), in_specs=[pl.BlockSpec(mem...  3.75 us
    ppermute x1, starting transfers between devices, per_device(): lax.ppermute(parts, 'feat', [(i, i ^ 1) for i in range(Y * Z * CORES)])  1.91 us
  transfers between devices with their start and end apart: 4, of which 3 were waited for; matrix products, arithmetic and copies ran while one was open for 0% of the time, Pallas kernels for 0%

profile of v7, /device:TPU:32, one launch (start us, length us, event | category | flops | bytes accessed | tf_op | source)
XLA Modules:
  0.0 76.6 jit_solution(6966124297912645070)
XLA Ops:
  0.0 0.0 copy-start
  0.0 0.0 copy-start.1
  0.0 3.7 %shard_map.46 = (f32[104,128]{1,0:T(8,128)}, f32[64,512]{1,0:T(8,128)}) custom-call(s32[1]{0:T(128)} %bitcast.own, f32[1,512]{1,0:T(1,128)} %bitcast.24, bf16[192,8192]{1,0:T(8,128)(2,1)} %design_ref.3, bf16[64,8192]{1,0:T(8,128)(2,1)} %bitcast.22), custom_call_target="tpu_custom_call" | custom-call | flops 201326592 | bytes 4194304 | tf_op jit(solution)/shard_map/pallas_call | solution.py:75
  3.8 1.9 %collective-permute-start = (f32[1,104,128]{2,1,0:T(8,128)}, f32[1,104,128]{2,1,0:T(8,128)S(1)}, u32[]{:S(2)}, u32[]{:S(2)}) collective-permute-start(f32[1,104,128]{2,1,0:T(8,128)} %bitcast.23), channel_id=1, source_target_pairs={{0,1},{1,0},{2,3},{3,2},{4,5},{5,4},{6,7},{7,6},{8,9},{9,8},{10,11... | collective-permute-start | bytes 159752 | tf_op jit(solution)/shard_map/ppermute | solution.py:169
  5.7 1.4 %collective-permute-done = f32[1,104,128]{2,1,0:T(8,128)S(1)} collective-permute-done((f32[1,104,128]{2,1,0:T(8,128)}, f32[1,104,128]{2,1,0:T(8,128)S(1)}, u32[]{:S(2)}, u32[]{:S(2)}) %collective-permute-start) | collective-permute-done | bytes 53280 | tf_op jit(solution)/shard_map/ppermute | solution.py:169
  7.1 0.8 %add_bitcast_fusion = f32[104,128]{1,0:T(8,128)S(1)} fusion(f32[1,104,128]{2,1,0:T(8,128)S(1)} %collective-permute-done, f32[104,128]{1,0:T(8,128)} %get-tuple-element.15), kind=kLoop, calls=%fused_computation.11 | loop fusion | flops 13312 | bytes 159744 | tf_op jit(solution)/shard_map/broadcast_in_dim | solution.py:170
  7.9 10.7 %all_to_all.15.refs_0_ = f32[4,104,128]{2,1,0:T(8,128)S(1)} all-to-all(f32[4,104,128]{2,1,0:T(8,128)S(1)} %broadcast_in_dim.20), channel_id=1, replica_groups={{0,8,16,24},{1,9,17,25},{2,10,18,26},{3,11,19,27},{4,12,20,28},{5,13,21..., dimensions={0} | all-to-all | bytes 425984 | tf_op jit(solution)/shard_map/all_to_all | solution.py:170
  18.7 12.3 %all_to_all.16.parts_ref = f32[4,104,128]{2,1,0:T(8,128)S(1)} all-to-all(f32[4,104,128]{2,1,0:T(8,128)S(1)} %shard_map.47), channel_id=1, replica_groups={{0,2,4,6},{1,3,5,7},{8,10,12,14},{9,11,13,15},{16,18,20,22},{17,19,21,2..., dimensions={0} | all-to-all | bytes 425984 | tf_op jit(solution)/shard_map/all_to_all | solution.py:171
  30.9 0.0 copy-done
  30.9 0.0 copy-done.1
  30.9 0.9 %shard_map.48 = (f32[4,4,64,512]{3,2,1,0:T(8,128)S(1)}, f32[64,512]{1,0:T(8,128)S(1)}) custom-call(s32[1]{0:T(128)} %bitcast.own, f32[1,192]{1,0:T(1,128)S(1)} %bitcast.21, f32[4,104,128]{2,1,0:T(8,128)S(1)} %all_to_all.16.parts_ref, bf16[192,8192]{1,0:T(8,128)(2,1)S(1)} %copy-done), custom_call_target="tpu_custom_call" | custom-call | flops 201326592 | bytes 5242880 | tf_op jit(solution)/shard_map/pallas_call | solution.py:148
  31.8 0.3 convert_element_type.24
  32.1 0.0 copy-start.2
  32.1 15.9 %all_to_all.17 = f16[4,4,64,512]{3,2,1,0:T(8,128)(2,1)S(1)} all-to-all(f16[4,4,64,512]{3,2,1,0:T(8,128)(2,1)S(1)} %convert_element_type.24), channel_id=1, replica_groups={{0,64,32,96},{128,192,160,224},{256,320,288,352},{384,448,416,480},{1,6..., dimensions={0} | all-to-all | bytes 2097152 | tf_op jit(solution)/shard_map/all_to_all | solution.py:174
  48.0 0.2 convert_reduce_fusion
  48.3 13.0 %collective-permute-start.1 = (f16[64,512]{1,0:T(8,128)(2,1)S(1)}, f16[64,512]{1,0:T(8,128)(2,1)S(1)}, u32[]{:S(2)}, u32[]{:S(2)}) collective-permute-start(f16[64,512]{1,0:T(8,128)(2,1)S(1)} %get-tuple-element.19), channel_id=1, source_target_pairs={{0,256},{32,288},{64,320},{96,352},{128,384},{160,416},{192,448},{... | collective-permute-start | bytes 196616 | tf_op jit(solution)/shard_map/ppermute | solution.py:179
  61.3 3.3 %collective-permute-start.3 = (f16[64,512]{1,0:T(8,128)(2,1)S(1)}, f16[64,512]{1,0:T(8,128)(2,1)S(1)}, u32[]{:S(2)}, u32[]{:S(2)}) collective-permute-start(f16[64,512]{1,0:T(8,128)(2,1)S(1)} %get-tuple-element.20), channel_id=1, source_target_pairs={{0,384},{32,416},{64,448},{96,480},{128,0},{160,32},{192,64},{224,... | collective-permute-start | bytes 196616 | tf_op jit(solution)/shard_map/ppermute | solution.py:179
  64.7 6.4 %collective-permute-start.2 = (f16[64,512]{1,0:T(8,128)(2,1)S(1)}, f16[64,512]{1,0:T(8,128)(2,1)S(1)}, u32[]{:S(2)}, u32[]{:S(2)}) collective-permute-start(f16[64,512]{1,0:T(8,128)(2,1)S(1)} %get-tuple-element.21), channel_id=1, source_target_pairs={{0,128},{32,160},{64,192},{96,224},{128,256},{160,288},{192,320},{... | collective-permute-start | bytes 196616 | tf_op jit(solution)/shard_map/ppermute | solution.py:179
  71.1 0.0 collective-permute-done.1
  71.1 1.9 %collective-permute-done.3 = f16[64,512]{1,0:T(8,128)(2,1)S(1)} collective-permute-done((f16[64,512]{1,0:T(8,128)(2,1)S(1)}, f16[64,512]{1,0:T(8,128)(2,1)S(1)}, u32[]{:S(2)}, u32[]{:S(2)}) %collective-permute-start.3) | collective-permute-done | bytes 65568 | tf_op jit(solution)/shard_map/ppermute | solution.py:179
  73.0 2.9 %collective-permute-done.2 = f16[64,512]{1,0:T(8,128)(2,1)S(1)} collective-permute-done((f16[64,512]{1,0:T(8,128)(2,1)S(1)}, f16[64,512]{1,0:T(8,128)(2,1)S(1)}, u32[]{:S(2)}, u32[]{:S(2)}) %collective-permute-start.2) | collective-permute-done | bytes 65568 | tf_op jit(solution)/shard_map/ppermute | solution.py:179
  75.9 0.0 copy-done.2
  75.9 0.7 fusion.4
  (4 shorter events, 0.1 us)
Async XLA Ops:
  0.0 30.9 %copy-start = (bf16[192,8192]{1,0:T(8,128)(2,1)S(1)}, bf16[192,8192]{1,0:T(8,128)(2,1)}, u32[]{:S(2)}) copy-start(bf16[192,8192]{1,0:T(8,128)(2,1)} %design_ref.3) | copy-start | bytes 9437188
  0.0 30.9 %copy-start.1 = (f32[192]{0:T(256)S(1)}, f32[192]{0:T(256)}, u32[]{:S(2)}) copy-start(f32[192]{0:T(256)} %param.5) | copy-start | bytes 2308
  3.8 3.3 %collective-permute-start = (f32[1,104,128]{2,1,0:T(8,128)}, f32[1,104,128]{2,1,0:T(8,128)S(1)}, u32[]{:S(2)}, u32[]{:S(2)}) collective-permute-start(f32[1,104,128]{2,1,0:T(8,128)} %bitcast.23), channel_id=1, source_target_pairs={{0,1},{1,0},{2,3},{3,2},{4,5},{5,4},{6,7},{7,6},{8,9},{9,8},{10,11... | collective-permute-start | bytes 159752 | tf_op jit(solution)/shard_map/ppermute | solution.py:169
  32.1 43.8 %copy-start.2 = (f32[64,512]{1,0:T(8,128)S(1)}, f32[64,512]{1,0:T(8,128)}, u32[]{:S(2)}) copy-start(f32[64,512]{1,0:T(8,128)} %get-tuple-element.18) | copy-start | bytes 393220
  48.3 22.8 %collective-permute-start.1 = (f16[64,512]{1,0:T(8,128)(2,1)S(1)}, f16[64,512]{1,0:T(8,128)(2,1)S(1)}, u32[]{:S(2)}, u32[]{:S(2)}) collective-permute-start(f16[64,512]{1,0:T(8,128)(2,1)S(1)} %get-tuple-element.19), channel_id=1, source_target_pairs={{0,256},{32,288},{64,320},{96,352},{128,384},{160,416},{192,448},{... | collective-permute-start | bytes 196616 | tf_op jit(solution)/shard_map/ppermute | solution.py:179
  61.3 11.7 %collective-permute-start.3 = (f16[64,512]{1,0:T(8,128)(2,1)S(1)}, f16[64,512]{1,0:T(8,128)(2,1)S(1)}, u32[]{:S(2)}, u32[]{:S(2)}) collective-permute-start(f16[64,512]{1,0:T(8,128)(2,1)S(1)} %get-tuple-element.20), channel_id=1, source_target_pairs={{0,384},{32,416},{64,448},{96,480},{128,0},{160,32},{192,64},{224,... | collective-permute-start | bytes 196616 | tf_op jit(solution)/shard_map/ppermute | solution.py:179
  64.7 11.2 %collective-permute-start.2 = (f16[64,512]{1,0:T(8,128)(2,1)S(1)}, f16[64,512]{1,0:T(8,128)(2,1)S(1)}, u32[]{:S(2)}, u32[]{:S(2)}) collective-permute-start(f16[64,512]{1,0:T(8,128)(2,1)S(1)} %get-tuple-element.21), channel_id=1, source_target_pairs={{0,128},{32,160},{64,192},{96,224},{128,256},{160,288},{192,320},{... | collective-permute-start | bytes 196616 | tf_op jit(solution)/shard_map/ppermute | solution.py:179

commit v8 on v6

--- a/solution.py
+++ b/solution.py
@@ -14,9 +14,10 @@
 WEIGHT_MAX = 0.25
 F16_TOP = 32768.0
 
-X_GROUPS = [[z * X + x for x in range(X)] for z in range(Z)]
+RING_ORDER = (0, 2, 1, 3)
+X_GROUPS = [[z * X + x for x in RING_ORDER] for z in range(Z)]
 FAR_FIRST = (2, 1, 3)
-Y_GROUPS = [[(y * Z + z) * CORES + c for y in range(Y)] for z in range(Z) for c in range(CORES)]
+Y_GROUPS = [[(y * Z + z) * CORES + c for y in RING_ORDER] for z in range(Z) for c in range(CORES)]
 ZLO_GROUPS = [[(y * Z + z) * CORES + c for z in range(Z)] for y in range(Y) for c in range(CORES)]
 
 VMEM = pl.BlockSpec(memory_space=pltpu.VMEM)
@@ -137,7 +138,7 @@
             part = lax.dot_general(
                 scaled, design_ref[:, at : at + owned], (((0,), (0,)), ((), ())), preferred_element_type=jnp.float32
             )
-            out_ref[x, lax.rem(z + Z - own_z, Z)] = part * down
+            out_ref[RING_ORDER.index(x), lax.rem(z + Z - own_z, Z)] = part * down
 
 
 def sketch_parts(own, weights, parts, design):

time: 77.2 us -> 76.6 us (level)
  no operation moved by 1% of the time
where the time goes in v8:
time: 76.6 us; the launch traced here: 76.3 us
  blocking collectives  38.6 us (50%)
  starting transfers between devices  24.7 us (32%)
  waiting for transfers between devices  6.17 us (8%)
  Pallas kernels  4.64 us (6%)
  other arithmetic  2.02 us (3%)
    ppermute x3, starting transfers between devices, per_device(): total += lax.ppermute(sent[far], 'samp', step).astype(jnp.float32)  22.8 us
    all_to_all x1, blocking collectives, per_device(): lax.all_to_all(sent.astype(jnp.float16), 'samp', 0, 0, axis_index_groups=...  15.9 us
    all_to_all x1, blocking collectives, per_device(): lax.all_to_all(resum(Z, parts), 'feat', 0, 0, axis_index_groups=ZLO_GROUPS)  12.2 us
    all_to_all x1, blocking collectives, per_device(): lax.all_to_all(jnp.broadcast_to(parts + other, (Y, *parts.shape[1:])), 'f...  10.5 us
    ppermute x3, waiting for transfers between devices, per_device(): total += lax.ppermute(sent[far], 'samp', step).astype(jnp.float32)  4.75 us
    pallas_call x1, Pallas kernels, project(): pl.pallas_call(project_kernel, grid=(CHUNKS,), in_specs=[pl.BlockSpec(mem...  3.75 us
    ppermute x1, starting transfers between devices, per_device(): lax.ppermute(parts, 'feat', [(i, i ^ 1) for i in range(Y * Z * CORES)])  1.91 us
  transfers between devices with their start and end apart: 4, of which 3 were waited for; matrix products, arithmetic and copies ran while one was open for 0% of the time, Pallas kernels for 0%

profile of v8, /device:TPU:32, one launch (start us, length us, event | category | flops | bytes accessed | tf_op | source)
XLA Modules:
  0.0 76.3 jit_solution(17274438270212077507)
XLA Ops:
  0.0 0.0 copy-start
  0.0 0.0 copy-start.1
  0.0 3.7 %shard_map.46 = (f32[104,128]{1,0:T(8,128)}, f32[64,512]{1,0:T(8,128)}) custom-call(s32[1]{0:T(128)} %bitcast.own, f32[1,512]{1,0:T(1,128)} %bitcast.24, bf16[192,8192]{1,0:T(8,128)(2,1)} %design_ref.3, bf16[64,8192]{1,0:T(8,128)(2,1)} %bitcast.22), custom_call_target="tpu_custom_call" | custom-call | flops 201326592 | bytes 4194304 | tf_op jit(solution)/shard_map/pallas_call | solution.py:75
  3.8 1.9 %collective-permute-start = (f32[1,104,128]{2,1,0:T(8,128)}, f32[1,104,128]{2,1,0:T(8,128)S(1)}, u32[]{:S(2)}, u32[]{:S(2)}) collective-permute-start(f32[1,104,128]{2,1,0:T(8,128)} %bitcast.23), channel_id=1, source_target_pairs={{0,1},{1,0},{2,3},{3,2},{4,5},{5,4},{6,7},{7,6},{8,9},{9,8},{10,11... | collective-permute-start | bytes 159752 | tf_op jit(solution)/shard_map/ppermute | solution.py:169
  5.7 1.4 %collective-permute-done = f32[1,104,128]{2,1,0:T(8,128)S(1)} collective-permute-done((f32[1,104,128]{2,1,0:T(8,128)}, f32[1,104,128]{2,1,0:T(8,128)S(1)}, u32[]{:S(2)}, u32[]{:S(2)}) %collective-permute-start) | collective-permute-done | bytes 53280 | tf_op jit(solution)/shard_map/ppermute | solution.py:169
  7.1 0.8 %add_bitcast_fusion = f32[104,128]{1,0:T(8,128)S(1)} fusion(f32[1,104,128]{2,1,0:T(8,128)S(1)} %collective-permute-done, f32[104,128]{1,0:T(8,128)} %get-tuple-element.15), kind=kLoop, calls=%fused_computation.11 | loop fusion | flops 13312 | bytes 159744 | tf_op jit(solution)/shard_map/broadcast_in_dim | solution.py:170
  7.9 10.5 %all_to_all.15.refs_0_ = f32[4,104,128]{2,1,0:T(8,128)S(1)} all-to-all(f32[4,104,128]{2,1,0:T(8,128)S(1)} %broadcast_in_dim.20), channel_id=1, replica_groups={{0,16,8,24},{1,17,9,25},{2,18,10,26},{3,19,11,27},{4,20,12,28},{5,21,13..., dimensions={0} | all-to-all | bytes 425984 | tf_op jit(solution)/shard_map/all_to_all | solution.py:170
  18.5 12.2 %all_to_all.16.parts_ref = f32[4,104,128]{2,1,0:T(8,128)S(1)} all-to-all(f32[4,104,128]{2,1,0:T(8,128)S(1)} %shard_map.47), channel_id=1, replica_groups={{0,2,4,6},{1,3,5,7},{8,10,12,14},{9,11,13,15},{16,18,20,22},{17,19,21,2..., dimensions={0} | all-to-all | bytes 425984 | tf_op jit(solution)/shard_map/all_to_all | solution.py:171
  30.6 0.0 copy-done
  30.6 0.0 copy-done.1
  30.6 0.9 %shard_map.48 = (f32[4,4,64,512]{3,2,1,0:T(8,128)S(1)}, f32[64,512]{1,0:T(8,128)S(1)}) custom-call(s32[1]{0:T(128)} %bitcast.own, f32[1,192]{1,0:T(1,128)S(1)} %bitcast.21, f32[4,104,128]{2,1,0:T(8,128)S(1)} %all_to_all.16.parts_ref, bf16[192,8192]{1,0:T(8,128)(2,1)S(1)} %copy-done), custom_call_target="tpu_custom_call" | custom-call | flops 201326592 | bytes 5242880 | tf_op jit(solution)/shard_map/pallas_call | solution.py:148
  31.5 0.3 convert_element_type.24
  31.8 0.0 copy-start.2
  31.8 15.9 %all_to_all.17 = f16[4,4,64,512]{3,2,1,0:T(8,128)(2,1)S(1)} all-to-all(f16[4,4,64,512]{3,2,1,0:T(8,128)(2,1)S(1)} %convert_element_type.24), channel_id=1, replica_groups={{0,64,32,96},{128,192,160,224},{256,320,288,352},{384,448,416,480},{1,6..., dimensions={0} | all-to-all | bytes 2097152 | tf_op jit(solution)/shard_map/all_to_all | solution.py:174
  47.7 0.2 convert_reduce_fusion
  48.0 13.0 %collective-permute-start.1 = (f16[64,512]{1,0:T(8,128)(2,1)S(1)}, f16[64,512]{1,0:T(8,128)(2,1)S(1)}, u32[]{:S(2)}, u32[]{:S(2)}) collective-permute-start(f16[64,512]{1,0:T(8,128)(2,1)S(1)} %get-tuple-element.19), channel_id=1, source_target_pairs={{0,256},{32,288},{64,320},{96,352},{128,384},{160,416},{192,448},{... | collective-permute-start | bytes 196616 | tf_op jit(solution)/shard_map/ppermute | solution.py:179
  61.0 3.3 %collective-permute-start.3 = (f16[64,512]{1,0:T(8,128)(2,1)S(1)}, f16[64,512]{1,0:T(8,128)(2,1)S(1)}, u32[]{:S(2)}, u32[]{:S(2)}) collective-permute-start(f16[64,512]{1,0:T(8,128)(2,1)S(1)} %get-tuple-element.20), channel_id=1, source_target_pairs={{0,384},{32,416},{64,448},{96,480},{128,0},{160,32},{192,64},{224,... | collective-permute-start | bytes 196616 | tf_op jit(solution)/shard_map/ppermute | solution.py:179
  64.4 6.4 %collective-permute-start.2 = (f16[64,512]{1,0:T(8,128)(2,1)S(1)}, f16[64,512]{1,0:T(8,128)(2,1)S(1)}, u32[]{:S(2)}, u32[]{:S(2)}) collective-permute-start(f16[64,512]{1,0:T(8,128)(2,1)S(1)} %get-tuple-element.21), channel_id=1, source_target_pairs={{0,128},{32,160},{64,192},{96,224},{128,256},{160,288},{192,320},{... | collective-permute-start | bytes 196616 | tf_op jit(solution)/shard_map/ppermute | solution.py:179
  70.8 0.0 collective-permute-done.1
  70.8 1.8 %collective-permute-done.3 = f16[64,512]{1,0:T(8,128)(2,1)S(1)} collective-permute-done((f16[64,512]{1,0:T(8,128)(2,1)S(1)}, f16[64,512]{1,0:T(8,128)(2,1)S(1)}, u32[]{:S(2)}, u32[]{:S(2)}) %collective-permute-start.3) | collective-permute-done | bytes 65568 | tf_op jit(solution)/shard_map/ppermute | solution.py:179
  72.6 2.9 %collective-permute-done.2 = f16[64,512]{1,0:T(8,128)(2,1)S(1)} collective-permute-done((f16[64,512]{1,0:T(8,128)(2,1)S(1)}, f16[64,512]{1,0:T(8,128)(2,1)S(1)}, u32[]{:S(2)}, u32[]{:S(2)}) %collective-permute-start.2) | collective-permute-done | bytes 65568 | tf_op jit(solution)/shard_map/ppermute | solution.py:179
  75.6 0.0 copy-done.2
  75.6 0.7 fusion.4
  (4 shorter events, 0.1 us)
Async XLA Ops:
  0.0 30.6 %copy-start = (bf16[192,8192]{1,0:T(8,128)(2,1)S(1)}, bf16[192,8192]{1,0:T(8,128)(2,1)}, u32[]{:S(2)}) copy-start(bf16[192,8192]{1,0:T(8,128)(2,1)} %design_ref.3) | copy-start | bytes 9437188
  0.0 30.6 %copy-start.1 = (f32[192]{0:T(256)S(1)}, f32[192]{0:T(256)}, u32[]{:S(2)}) copy-start(f32[192]{0:T(256)} %param.5) | copy-start | bytes 2308
  3.8 3.3 %collective-permute-start = (f32[1,104,128]{2,1,0:T(8,128)}, f32[1,104,128]{2,1,0:T(8,128)S(1)}, u32[]{:S(2)}, u32[]{:S(2)}) collective-permute-start(f32[1,104,128]{2,1,0:T(8,128)} %bitcast.23), channel_id=1, source_target_pairs={{0,1},{1,0},{2,3},{3,2},{4,5},{5,4},{6,7},{7,6},{8,9},{9,8},{10,11... | collective-permute-start | bytes 159752 | tf_op jit(solution)/shard_map/ppermute | solution.py:169
  31.8 43.8 %copy-start.2 = (f32[64,512]{1,0:T(8,128)S(1)}, f32[64,512]{1,0:T(8,128)}, u32[]{:S(2)}) copy-start(f32[64,512]{1,0:T(8,128)} %get-tuple-element.18) | copy-start | bytes 393220
  48.0 22.8 %collective-permute-start.1 = (f16[64,512]{1,0:T(8,128)(2,1)S(1)}, f16[64,512]{1,0:T(8,128)(2,1)S(1)}, u32[]{:S(2)}, u32[]{:S(2)}) collective-permute-start(f16[64,512]{1,0:T(8,128)(2,1)S(1)} %get-tuple-element.19), channel_id=1, source_target_pairs={{0,256},{32,288},{64,320},{96,352},{128,384},{160,416},{192,448},{... | collective-permute-start | bytes 196616 | tf_op jit(solution)/shard_map/ppermute | solution.py:179
  61.0 11.6 %collective-permute-start.3 = (f16[64,512]{1,0:T(8,128)(2,1)S(1)}, f16[64,512]{1,0:T(8,128)(2,1)S(1)}, u32[]{:S(2)}, u32[]{:S(2)}) collective-permute-start(f16[64,512]{1,0:T(8,128)(2,1)S(1)} %get-tuple-element.20), channel_id=1, source_target_pairs={{0,384},{32,416},{64,448},{96,480},{128,0},{160,32},{192,64},{224,... | collective-permute-start | bytes 196616 | tf_op jit(solution)/shard_map/ppermute | solution.py:179
  64.4 11.2 %collective-permute-start.2 = (f16[64,512]{1,0:T(8,128)(2,1)S(1)}, f16[64,512]{1,0:T(8,128)(2,1)S(1)}, u32[]{:S(2)}, u32[]{:S(2)}) collective-permute-start(f16[64,512]{1,0:T(8,128)(2,1)S(1)} %get-tuple-element.21), channel_id=1, source_target_pairs={{0,128},{32,160},{64,192},{96,224},{128,256},{160,288},{192,320},{... | collective-permute-start | bytes 196616 | tf_op jit(solution)/shard_map/ppermute | solution.py:179
